TPU v7x, 256 devices: a whole 4x4x8 slice. The times are simulated.
256 devices in a mesh: dp: 4 (over y), pipe: 4 (over x), tensor: 16 (over z, core).
Axes of the slice: x: 4, y: 4, z: 8, core: 2. Of those that a mesh axis runs over, the one named last changes fastest.
Arguments:
- tokens: bfloat16 [2048, 3072], P(('dp', 'tensor')), may hold values from -6 to 6
- destination: int32 [2048], P(('dp', 'tensor')), may hold values from 0 to 2047, as said below
- segments: int32 [16, 128], P('dp'), may hold values from 0 to 5, never falling along the last dimension, each value on 1 to 64 neighbouring positions
- query_weight: bfloat16 [4, 3072, 2048], P('pipe', None, 'tensor')
- key_value_weight: bfloat16 [4, 3072, 2048], P('pipe', None, 'tensor')
- out_weight: bfloat16 [4, 2048, 3072], P('pipe', 'tensor'), may hold values from -0.125 to 0.125
- gate_weight: bfloat16 [4, 3072, 8192], P('pipe', None, 'tensor'), may hold values from -0.109375 to 0.109375
- up_weight: bfloat16 [4, 3072, 8192], P('pipe', None, 'tensor'), may hold values from -0.109375 to 0.109375
- down_weight: bfloat16 [4, 8192, 3072], P('pipe', 'tensor'), may hold values from -0.0625 to 0.0625
- attention_gain: float32 [4, 3072], P('pipe'), may hold values from 0.1 to 1.9
- forward_gain: float32 [4, 3072], P('pipe'), may hold values from 0.1 to 1.9
Outputs:
- layers_out: float32 [2048, 3072], P(('dp', 'pipe', 'tensor'))
Inputs may be any that keep to these rules, and one draw needn't show every extreme that they name: destination is a permutation of the 2048 rows. A row held at tensor index t goes to a place within its micro-batch in [t * 8, (t + 1) * 8). At most 16 rows of one device go to one dp index, and every device sends exactly 16 rows to some dp index.
All inputs are finite; a program needn't handle non-finite values.
Results may differ from a plain program's by a relative error of at most 0.04.
Values may be sent and summed in bfloat16 or wider, within the bound.
No kernel may reach another device: no remote copies, remote signals or barrier semaphores. Data moves between devices by JAX's collectives and lax.ppermute only.
A program may use at most 64 MiB of HBM per device.

v0:
```python
import jax
import jax.numpy as jnp
from jax import lax
from jax.sharding import PartitionSpec as P

HD = 128


def swapped(value, axis, apart):
    mask = 2**apart
    pairs = [(source, source ^ mask) for source in range(lax.axis_size(axis))]
    return lax.ppermute(value, axis, pairs)


def shifted(array, axis, by):
    peers = lax.axis_size(axis)
    pairs = [(i, i + by) for i in range(peers) if 0 <= i + by < peers]
    return lax.ppermute(array, axis, pairs)


def broadcast(block, axis, source):
    block = jnp.where(lax.axis_index(axis) == source, block, jnp.zeros_like(block))
    return lax.psum(block, axis)


def doc_positions(doc_ids):
    order = jnp.arange(doc_ids.shape[0], dtype=jnp.int32)
    change = jnp.concatenate([jnp.ones((1,), dtype=bool), doc_ids[1:] != doc_ids[:-1]])
    starts = lax.cummax(jnp.where(change, order, jnp.zeros_like(order)), axis=0)
    return (order - starts).astype(jnp.float32)


def rotate(stack, places):
    half_width = stack.shape[-1] // 2
    frequency = 500000.0 ** (-(jnp.arange(half_width, dtype=jnp.float32) * 2.0 / stack.shape[-1]))
    angles = places[:, None] * frequency[None, :]
    cosine = jnp.cos(angles)[:, None, :]
    sine_part = jnp.sin(angles)[:, None, :]
    front_half = stack[..., :half_width]
    back_half = stack[..., half_width:]
    return jnp.concatenate(
        [front_half * cosine - back_half * sine_part, back_half * cosine + front_half * sine_part],
        axis=-1,
    )


def normalize(rows_in, gain):
    meansq = jnp.mean(rows_in * rows_in, axis=-1, keepdims=True)
    return (rows_in * lax.rsqrt(meansq + 1e-05) * gain).astype(jnp.bfloat16)


def visible(doc_ids):
    order = jnp.arange(doc_ids.shape[0], dtype=jnp.int32)
    return jnp.logical_and(doc_ids[:, None] == doc_ids[None, :], order[None, :] <= order[:, None])


def attend(queries, key_heads, value_heads, doc_ids):
    rows, heads_here, head_width = queries.shape
    shared_heads = key_heads.shape[1]
    grouped_queries = queries.reshape(rows, shared_heads, heads_here // shared_heads, head_width)
    scores = jnp.einsum(
        "qagd,kad->agqk",
        grouped_queries,
        key_heads,
        precision=lax.Precision.HIGHEST,
        preferred_element_type=jnp.float32,
    ) * head_width ** (-0.5)
    scores = jnp.where(visible(doc_ids), scores, jnp.float32(-1e30))
    row_max = jnp.max(scores, axis=-1, keepdims=True)
    spread = jnp.exp(scores - row_max)
    weights = (spread / jnp.sum(spread, axis=-1, keepdims=True)).astype(jnp.bfloat16)
    mixed = jnp.einsum("agqk,kad->qagd", weights, value_heads, preferred_element_type=jnp.float32)
    return mixed.astype(jnp.bfloat16).reshape(rows, heads_here * head_width)


def expand(rows_in, gate_local, up_local):
    gate = jnp.dot(rows_in, gate_local, preferred_element_type=jnp.float32)
    upward = jnp.dot(rows_in, up_local, preferred_element_type=jnp.float32)
    return (jax.nn.silu(gate) * upward).astype(jnp.bfloat16)


def split_pairs(pairs, places):
    rows = pairs.shape[0]
    parity = lax.axis_index("tensor") % 2
    turned = rotate(pairs.reshape(rows, 1, HD), places).reshape(rows, HD)
    mine = jnp.where(parity == 0, turned, pairs)
    partner = swapped(mine.astype(jnp.bfloat16), "tensor", 0).astype(mine.dtype)
    key_heads = jnp.where(parity == 0, mine, partner).reshape(rows, 1, HD)
    value_heads = jnp.where(parity == 0, partner, mine).astype(jnp.bfloat16).reshape(rows, 1, HD)
    return (key_heads, value_heads)


def run_layer(current, doc_ids, layer_weights):
    (
        query_local,
        pair_local,
        out_local,
        gate_local,
        up_local,
        down_local,
        gain_attention,
        gain_forward,
    ) = layer_weights
    micro_rows = doc_ids.shape[0]
    query_cols = query_local.shape[1]
    places = doc_positions(doc_ids)
    piece = lax.all_gather(normalize(current, gain_attention), "tensor", axis=0, tiled=True)
    projected = jnp.concatenate(
        [
            jnp.dot(piece, query_local, preferred_element_type=jnp.float32),
            jnp.dot(piece, pair_local, preferred_element_type=jnp.float32),
        ],
        axis=1,
    )
    heads_here = query_cols // HD
    queries = rotate(projected[:, :query_cols].reshape(micro_rows, heads_here, HD), places)
    key_heads, value_heads = split_pairs(projected[:, query_cols:], places)
    mixed = attend(queries, key_heads, value_heads, doc_ids)
    total = lax.psum_scatter(
        jnp.dot(mixed, out_local, preferred_element_type=jnp.float32).astype(jnp.bfloat16),
        "tensor",
        scatter_dimension=0,
        tiled=True,
    ).astype(jnp.float32)
    halfway = current + total
    hidden = expand(
        lax.all_gather(normalize(halfway, gain_forward), "tensor", axis=0, tiled=True),
        gate_local,
        up_local,
    )
    forward = lax.psum_scatter(
        jnp.dot(hidden, down_local, preferred_element_type=jnp.float32).astype(jnp.bfloat16),
        "tensor",
        scatter_dimension=0,
        tiled=True,
    ).astype(jnp.float32)
    return halfway + forward


def pass_on(result):
    return shifted(result.astype(jnp.bfloat16), "pipe", 1).astype(result.dtype)


def shards(
    tokens,
    destination,
    segments,
    query_weight,
    key_value_weight,
    out_weight,
    gate_weight,
    up_weight,
    down_weight,
    attention_gain,
    forward_gain,
):
    group_count = lax.axis_size("dp")
    tensor_count = lax.axis_size("tensor")
    pipe_count = lax.axis_size("pipe")
    micro_count, micro_rows = segments.shape
    slab_rows = micro_rows // tensor_count
    held_rows, width = tokens.shape
    capacity = held_rows // 2
    group_span = micro_count * micro_rows
    target = destination // group_span
    within = destination % group_span
    landing = within // micro_rows * slab_rows + within % slab_rows
    member = (target[:, None] == jnp.arange(group_count, dtype=jnp.int32)[None, :]).astype(
        jnp.int32
    )
    before = jnp.sum((jnp.cumsum(member, axis=0) - member) * member, axis=1)
    slot_index = target * capacity + before
    send_rows = jnp.zeros((group_count * capacity, width), jnp.bfloat16).at[slot_index].set(tokens)
    send_places = (
        jnp.full((group_count * capacity,), held_rows, jnp.int32).at[slot_index].set(landing)
    )
    got_rows, got_places = (
        lax.all_to_all(
            send_rows.reshape(group_count, capacity, width),
            "dp",
            split_axis=0,
            concat_axis=0,
            tiled=True,
        ),
        lax.all_to_all(
            send_places.reshape(group_count, capacity),
            "dp",
            split_axis=0,
            concat_axis=0,
            tiled=True,
        ),
    )
    regrouped = (
        jnp.zeros((held_rows, width), jnp.bfloat16)
        .at[got_places.reshape(-1)]
        .set(got_rows.reshape(-1, width), mode="drop")
    )
    micro_batches = regrouped.reshape(micro_count, slab_rows, width)
    layer_weights = (
        query_weight[0],
        key_value_weight[0],
        out_weight[0],
        gate_weight[0],
        up_weight[0],
        down_weight[0],
        attention_gain[0],
        forward_gain[0],
    )
    phase_index = lax.axis_index("pipe")
    carried = jnp.zeros((slab_rows, width), jnp.float32)
    finished = []
    for moment in range(micro_count + pipe_count - 1):
        feed_rows = micro_batches[min(moment, micro_count - 1)].astype(jnp.float32)
        current = jnp.where(
            jnp.logical_and(phase_index == 0, moment < micro_count), feed_rows, carried
        )
        micro_index = jnp.clip(moment - phase_index, 0, micro_count - 1)
        doc_ids = lax.dynamic_index_in_dim(segments, micro_index, 0, keepdims=False)
        result = run_layer(current, doc_ids, layer_weights)
        if moment >= pipe_count - 1:
            finished.append(result)
        if moment < micro_count + pipe_count - 2:
            carried = pass_on(result)
    everyone = broadcast(jnp.stack(finished).astype(jnp.bfloat16), "pipe", pipe_count - 1).astype(
        jnp.float32
    )
    return lax.dynamic_index_in_dim(everyone, phase_index, 0, keepdims=False)


def solution(mesh):
    placed = (
        P(("dp", "tensor"), None),
        P(("dp", "tensor")),
        P("dp", None),
        P("pipe", None, "tensor"),
        P("pipe", None, "tensor"),
        P("pipe", "tensor", None),
        P("pipe", None, "tensor"),
        P("pipe", None, "tensor"),
        P("pipe", "tensor", None),
        P("pipe", None),
        P("pipe", None),
    )
    return jax.shard_map(
        shards,
        mesh=mesh,
        in_specs=placed,
        out_specs=P(("dp", "pipe", "tensor"), None),
        check_vma=False,
    )
```

profile of v0, /device:TPU:7, one launch (start us, length us, event | category | flops | bytes accessed | tf_op | source)
XLA Modules:
  0.0 1276.3 jit_solution(13476651444609585286)
XLA Ops:
  32.3 24.7 %all_gather.42 = bf16[128,3072]{1,0:T(8,128)(2,1)S(1)} all-gather(bf16[8,3072]{1,0:T(8,128)(2,1)S(1)} %multiply_convert_fusion.10), channel_id=1, replica_groups=mesh['dp'=4,'pipe'=4,'tensor'=16] {'tensor'}, dimensions={0}, use_global_device_ids=true | all-gather | bytes 835584 | tf_op jit(solution)/shard_map/all_gather | solution.py:107
  65.5 49.7 %reduce-scatter.15.cloned.1.call-done = bf16[8,3072]{1,0:T(8,128)(2,1)} async-done(((bf16[128,3072]{1,0:T(8,128)(2,1)}), bf16[8,3072]{1,0:T(8,128)(2,1)}) %reduce-scatter.15.cloned.1.call-update) | async-done | bytes 49168 | tf_op jit(solution)/shard_map/reduce_scatter | solution.py:119
  145.7 52.2 %reduce-scatter.17.cloned.1.call-done = bf16[8,3072]{1,0:T(8,128)(2,1)} async-done(((bf16[128,3072]{1,0:T(8,128)(2,1)}), bf16[8,3072]{1,0:T(8,128)(2,1)}) %reduce-scatter.17.cloned.1.call-update) | async-done | bytes 49168 | tf_op jit(solution)/shard_map/reduce_scatter | solution.py:131
  203.9 21.2 %all_gather.44 = bf16[128,3072]{1,0:T(8,128)(2,1)S(1)} all-gather(bf16[8,3072]{1,0:T(8,128)(2,1)S(1)} %multiply_convert_fusion.8), channel_id=1, replica_groups=mesh['dp'=4,'pipe'=4,'tensor'=16] {'tensor'}, dimensions={0}, use_global_device_ids=true | all-gather | bytes 835584 | tf_op jit(solution)/shard_map/all_gather | solution.py:107
  234.6 52.2 %reduce-scatter.19.cloned.1.call-done = bf16[8,3072]{1,0:T(8,128)(2,1)} async-done(((bf16[128,3072]{1,0:T(8,128)(2,1)}), bf16[8,3072]{1,0:T(8,128)(2,1)}) %reduce-scatter.19.cloned.1.call-update) | async-done | bytes 49168 | tf_op jit(solution)/shard_map/reduce_scatter | solution.py:119
  288.7 20.1 %all_gather.45 = bf16[128,3072]{1,0:T(8,128)(2,1)S(1)} all-gather(bf16[8,3072]{1,0:T(8,128)(2,1)S(1)} %multiply_convert_fusion.7), channel_id=1, replica_groups=mesh['dp'=4,'pipe'=4,'tensor'=16] {'tensor'}, dimensions={0}, use_global_device_ids=true | all-gather | bytes 835584 | tf_op jit(solution)/shard_map/all_gather | solution.py:127
  319.7 49.6 %reduce-scatter.21.cloned.1.call-done = bf16[8,3072]{1,0:T(8,128)(2,1)} async-done(((bf16[128,3072]{1,0:T(8,128)(2,1)}), bf16[8,3072]{1,0:T(8,128)(2,1)}) %reduce-scatter.21.cloned.1.call-update) | async-done | bytes 49168 | tf_op jit(solution)/shard_map/reduce_scatter | solution.py:131
  375.2 21.3 %all_gather.46 = bf16[128,3072]{1,0:T(8,128)(2,1)S(1)} all-gather(bf16[8,3072]{1,0:T(8,128)(2,1)S(1)} %multiply_convert_fusion.6), channel_id=1, replica_groups=mesh['dp'=4,'pipe'=4,'tensor'=16] {'tensor'}, dimensions={0}, use_global_device_ids=true | all-gather | bytes 835584 | tf_op jit(solution)/shard_map/all_gather | solution.py:107
  406.0 52.6 %reduce-scatter.23.cloned.1.call-done = bf16[8,3072]{1,0:T(8,128)(2,1)} async-done(((bf16[128,3072]{1,0:T(8,128)(2,1)}), bf16[8,3072]{1,0:T(8,128)(2,1)}) %reduce-scatter.23.cloned.1.call-update) | async-done | bytes 49168 | tf_op jit(solution)/shard_map/reduce_scatter | solution.py:119
  490.6 50.6 %reduce-scatter.25.cloned.1.call-done = bf16[8,3072]{1,0:T(8,128)(2,1)} async-done(((bf16[128,3072]{1,0:T(8,128)(2,1)}), bf16[8,3072]{1,0:T(8,128)(2,1)}) %reduce-scatter.25.cloned.1.call-update) | async-done | bytes 49168 | tf_op jit(solution)/shard_map/reduce_scatter | solution.py:131
  547.2 21.2 %all_gather.48 = bf16[128,3072]{1,0:T(8,128)(2,1)S(1)} all-gather(bf16[8,3072]{1,0:T(8,128)(2,1)S(1)} %multiply_convert_fusion.4), channel_id=1, replica_groups=mesh['dp'=4,'pipe'=4,'tensor'=16] {'tensor'}, dimensions={0}, use_global_device_ids=true | all-gather | bytes 835584 | tf_op jit(solution)/shard_map/all_gather | solution.py:107
  577.8 52.2 %reduce-scatter.27.cloned.1.call-done = bf16[8,3072]{1,0:T(8,128)(2,1)} async-done(((bf16[128,3072]{1,0:T(8,128)(2,1)}), bf16[8,3072]{1,0:T(8,128)(2,1)}) %reduce-scatter.27.cloned.1.call-update) | async-done | bytes 49168 | tf_op jit(solution)/shard_map/reduce_scatter | solution.py:119
  662.8 49.9 %reduce-scatter.29.cloned.1.call-done = bf16[8,3072]{1,0:T(8,128)(2,1)} async-done(((bf16[128,3072]{1,0:T(8,128)(2,1)}), bf16[8,3072]{1,0:T(8,128)(2,1)}) %reduce-scatter.29.cloned.1.call-update) | async-done | bytes 49168 | tf_op jit(solution)/shard_map/reduce_scatter | solution.py:131
  718.6 21.2 %all_gather.50 = bf16[128,3072]{1,0:T(8,128)(2,1)S(1)} all-gather(bf16[8,3072]{1,0:T(8,128)(2,1)S(1)} %fusion.186), channel_id=1, replica_groups=mesh['dp'=4,'pipe'=4,'tensor'=16] {'tensor'}, dimensions={0}, use_global_device_ids=true | all-gather | bytes 835584 | tf_op jit(solution)/shard_map/all_gather | solution.py:107
  748.2 52.2 %reduce-scatter.31.cloned.1.call-done = bf16[8,3072]{1,0:T(8,128)(2,1)} async-done(((bf16[128,3072]{1,0:T(8,128)(2,1)}), bf16[8,3072]{1,0:T(8,128)(2,1)}) %reduce-scatter.31.cloned.1.call-update) | async-done | bytes 49168 | tf_op jit(solution)/shard_map/reduce_scatter | solution.py:119
  802.3 20.2 %all_gather.51 = bf16[128,3072]{1,0:T(8,128)(2,1)S(1)} all-gather(bf16[8,3072]{1,0:T(8,128)(2,1)S(1)} %multiply_convert_fusion.2), channel_id=1, replica_groups=mesh['dp'=4,'pipe'=4,'tensor'=16] {'tensor'}, dimensions={0}, use_global_device_ids=true | all-gather | bytes 835584 | tf_op jit(solution)/shard_map/all_gather | solution.py:127
  830.5 52.2 %reduce-scatter.33.cloned.1.call-done = bf16[8,3072]{1,0:T(8,128)(2,1)} async-done(((bf16[128,3072]{1,0:T(8,128)(2,1)}), bf16[8,3072]{1,0:T(8,128)(2,1)}) %reduce-scatter.33.cloned.1.call-update) | async-done | bytes 49168 | tf_op jit(solution)/shard_map/reduce_scatter | solution.py:131
  888.6 21.2 %all_gather.52 = bf16[128,3072]{1,0:T(8,128)(2,1)S(1)} all-gather(bf16[8,3072]{1,0:T(8,128)(2,1)S(1)} %fusion.189), channel_id=1, replica_groups=mesh['dp'=4,'pipe'=4,'tensor'=16] {'tensor'}, dimensions={0}, use_global_device_ids=true | all-gather | bytes 835584 | tf_op jit(solution)/shard_map/all_gather | solution.py:107
  918.2 52.2 %reduce-scatter.35.cloned.1.call-done = bf16[8,3072]{1,0:T(8,128)(2,1)} async-done(((bf16[128,3072]{1,0:T(8,128)(2,1)}), bf16[8,3072]{1,0:T(8,128)(2,1)}) %reduce-scatter.35.cloned.1.call-update) | async-done | bytes 49168 | tf_op jit(solution)/shard_map/reduce_scatter | solution.py:119
  1000.4 51.9 %reduce-scatter.37.cloned.1.call-done = bf16[8,3072]{1,0:T(8,128)(2,1)} async-done(((bf16[128,3072]{1,0:T(8,128)(2,1)}), bf16[8,3072]{1,0:T(8,128)(2,1)}) %reduce-scatter.37.cloned.1.call-update) | async-done | bytes 49168 | tf_op jit(solution)/shard_map/reduce_scatter | solution.py:131
  1058.3 21.2 %all_gather.54 = bf16[128,3072]{1,0:T(8,128)(2,1)S(1)} all-gather(bf16[8,3072]{1,0:T(8,128)(2,1)S(1)} %fusion.192), channel_id=1, replica_groups=mesh['dp'=4,'pipe'=4,'tensor'=16] {'tensor'}, dimensions={0}, use_global_device_ids=true | all-gather | bytes 835584 | tf_op jit(solution)/shard_map/all_gather | solution.py:107
  1087.1 52.1 %reduce-scatter.39.cloned.1.call-done = bf16[8,3072]{1,0:T(8,128)(2,1)} async-done(((bf16[128,3072]{1,0:T(8,128)(2,1)}), bf16[8,3072]{1,0:T(8,128)(2,1)}) %reduce-scatter.39.cloned.1.call-update) | async-done | bytes 49168 | tf_op jit(solution)/shard_map/reduce_scatter | solution.py:119
  1168.7 52.4 %reduce-scatter.41.cloned.1.call-done = bf16[8,3072]{1,0:T(8,128)(2,1)} async-done(((bf16[128,3072]{1,0:T(8,128)(2,1)}), bf16[8,3072]{1,0:T(8,128)(2,1)}) %reduce-scatter.41.cloned.1.call-update) | async-done | bytes 49168 | tf_op jit(solution)/shard_map/reduce_scatter | solution.py:131
  1223.4 44.9 %all-reduce.2.cloned.1.call-done = bf16[4,8,3072]{2,1,0:T(8,128)(2,1)} async-done(((bf16[4,8,3072]{2,1,0:T(8,128)(2,1)}), bf16[4,8,3072]{2,1,0:T(8,128)(2,1)}) %all-reduce.2.cloned.1.call-update) | async-done | bytes 196624 | tf_op jit(solution)/shard_map/psum | solution.py:23
  (325 shorter events, 302.9 us)
Async XLA Ops:
  9.0 9.4 all-to-all-start
  18.5 10.5 all-to-all-start.1
  22.7 92.5 %reduce-scatter.15.cloned.1.call-start = ((), (), s32[]{:S(2)}) async-start(), calls=%async_computation.16 | async-start | bytes 835584 | tf_op jit(solution)/shard_map/reduce_scatter | solution.py:119
  60.4 1.3 collective-permute-start
  65.4 132.5 %reduce-scatter.17.cloned.1.call-start = ((), (), s32[]{:S(2)}) async-start(), calls=%async_computation.17 | async-start | bytes 835584 | tf_op jit(solution)/shard_map/reduce_scatter | solution.py:131
  145.3 141.6 %reduce-scatter.19.cloned.1.call-start = ((), (), s32[]{:S(2)}) async-start(), calls=%async_computation.18 | async-start | bytes 835584 | tf_op jit(solution)/shard_map/reduce_scatter | solution.py:119
  198.8 4.8 collective-permute-start.1
  234.6 134.7 %reduce-scatter.21.cloned.1.call-start = ((), (), s32[]{:S(2)}) async-start(), calls=%async_computation.19 | async-start | bytes 835584 | tf_op jit(solution)/shard_map/reduce_scatter | solution.py:131
  317.0 141.6 %reduce-scatter.23.cloned.1.call-start = ((), (), s32[]{:S(2)}) async-start(), calls=%async_computation.20 | async-start | bytes 835584 | tf_op jit(solution)/shard_map/reduce_scatter | solution.py:119
  370.1 4.8 collective-permute-start.3
  406.0 135.3 %reduce-scatter.25.cloned.1.call-start = ((), (), s32[]{:S(2)}) async-start(), calls=%async_computation.21 | async-start | bytes 835584 | tf_op jit(solution)/shard_map/reduce_scatter | solution.py:131
  488.8 141.3 %reduce-scatter.27.cloned.1.call-start = ((), (), s32[]{:S(2)}) async-start(), calls=%async_computation.22 | async-start | bytes 835584 | tf_op jit(solution)/shard_map/reduce_scatter | solution.py:119
  542.1 4.8 collective-permute-start.5
  577.8 134.9 %reduce-scatter.29.cloned.1.call-start = ((), (), s32[]{:S(2)}) async-start(), calls=%async_computation.23 | async-start | bytes 835584 | tf_op jit(solution)/shard_map/reduce_scatter | solution.py:131
  660.2 140.3 %reduce-scatter.31.cloned.1.call-start = ((), (), s32[]{:S(2)}) async-start(), calls=%async_computation.24 | async-start | bytes 835584 | tf_op jit(solution)/shard_map/reduce_scatter | solution.py:119
  713.5 4.8 collective-permute-start.7
  748.1 134.6 %reduce-scatter.33.cloned.1.call-start = ((), (), s32[]{:S(2)}) async-start(), calls=%async_computation.25 | async-start | bytes 835584 | tf_op jit(solution)/shard_map/reduce_scatter | solution.py:131
  830.0 140.4 %reduce-scatter.35.cloned.1.call-start = ((), (), s32[]{:S(2)}) async-start(), calls=%async_computation.26 | async-start | bytes 835584 | tf_op jit(solution)/shard_map/reduce_scatter | solution.py:119
  883.6 4.8 collective-permute-start.9
  918.1 134.2 %reduce-scatter.37.cloned.1.call-start = ((), (), s32[]{:S(2)}) async-start(), calls=%async_computation.27 | async-start | bytes 835584 | tf_op jit(solution)/shard_map/reduce_scatter | solution.py:131
  999.8 139.3 %reduce-scatter.39.cloned.1.call-start = ((), (), s32[]{:S(2)}) async-start(), calls=%async_computation.28 | async-start | bytes 835584 | tf_op jit(solution)/shard_map/reduce_scatter | solution.py:119
  1053.2 4.8 collective-permute-start.11
  1087.1 134.0 %reduce-scatter.41.cloned.1.call-start = ((), (), s32[]{:S(2)}) async-start(), calls=%async_computation.29 | async-start | bytes 835584 | tf_op jit(solution)/shard_map/reduce_scatter | solution.py:131
  1168.6 99.8 %all-reduce.2.cloned.1.call-start = ((), (), s32[]{:S(2)}) async-start(), calls=%async_computation.30 | async-start | bytes 393216 | tf_op jit(solution)/shard_map/psum | solution.py:23
  (52 other events, 800.5 us)
Sparse Core Ops, SparseCore 0:
  65.6 49.5 reduce-scatter.14
  145.4 52.5 reduce-scatter.16
  234.7 52.1 reduce-scatter.18
  317.1 52.1 reduce-scatter.20
  406.1 52.4 reduce-scatter.22
  488.9 52.3 reduce-scatter.24
  577.9 52.0 reduce-scatter.26
  660.3 52.3 reduce-scatter.28
  748.2 52.1 reduce-scatter.30
  830.2 52.5 reduce-scatter.32
  918.3 52.1 reduce-scatter.34
  1000.0 52.3 reduce-scatter.36
  1087.2 51.9 reduce-scatter.38
  1168.7 52.2 reduce-scatter.40
  1223.6 44.7 all-reduce.1
where the time goes:
time: 1280 us
  waiting for transfers between devices  801 us (63%)
  blocking collectives  292 us (23%)
  matrix products  95.4 us (7%)
  other arithmetic  38.4 us (3%)
  starting transfers between devices  18.5 us (1%)
  local copies, waits for them, and re-layouts  16.7 us (1%)
  between operations  14.1 us (1%)
    reduce_scatter x7, waiting for transfers between devices, run_layer(): lax.psum_scatter(jnp.dot(mixed, out_local, preferred_element_type=jnp.flo...  363 us
    reduce_scatter x7, waiting for transfers between devices, run_layer(): lax.psum_scatter(jnp.dot(hidden, down_local, preferred_element_type=jnp.f...  359 us
    all_gather x7, blocking collectives, run_layer(): lax.all_gather(normalize(current, gain_attention), 'tensor', axis=0, tile...  152 us
    all_gather x7, blocking collectives, run_layer(): lax.all_gather(normalize(halfway, gain_forward), 'tensor', axis=0, tiled=...  140 us
    psum x1, waiting for transfers between devices, broadcast(): return lax.psum(block, axis)  44.9 us
    dot_general x7, matrix products, run_layer(): jnp.dot(hidden, down_local, preferred_element_type=jnp.float32)  28.9 us
  transfers between devices with their start and end apart: 30, of which 29 were waited for; matrix products, arithmetic and copies ran while one was open for 1% of the time, Pallas kernels for 0%

commit v1 on v0

--- a/solution.py
+++ b/solution.py
@@ -12,15 +12,32 @@
     return lax.ppermute(value, axis, pairs)
 
 
-def shifted(array, axis, by):
-    peers = lax.axis_size(axis)
-    pairs = [(i, i + by) for i in range(peers) if 0 <= i + by < peers]
-    return lax.ppermute(array, axis, pairs)
-
-
-def broadcast(block, axis, source):
-    block = jnp.where(lax.axis_index(axis) == source, block, jnp.zeros_like(block))
-    return lax.psum(block, axis)
+def same_core_groups():
+    peers = lax.axis_size("tensor")
+    return [list(range(core, peers, 2)) for core in range(2)]
+
+
+def scatter_sum(left, weight):
+    chips = lax.axis_size("tensor") // 2
+    rows = left.shape[0] // (2 * chips)
+    parity = lax.axis_index("tensor") % 2
+    split = left.reshape(chips, 2, rows, -1)
+    mine = jnp.where(parity == 0, split[:, 0], split[:, 1])
+    other = jnp.where(parity == 0, split[:, 1], split[:, 0])
+    ordered = jnp.concatenate([other, mine], axis=0).reshape(left.shape)
+    part = jnp.dot(ordered, weight, preferred_element_type=jnp.float32)
+    half = chips * rows
+    got = swapped(part[:half].astype(jnp.bfloat16), "tensor", 0)
+    pair = (part[half:] + got.astype(jnp.float32)).astype(jnp.bfloat16)
+    blocks = lax.all_to_all(
+        pair.reshape(chips, rows, -1),
+        "tensor",
+        split_axis=0,
+        concat_axis=0,
+        tiled=True,
+        axis_index_groups=same_core_groups(),
+    )
+    return jnp.sum(blocks.astype(jnp.float32), axis=0)
 
 
 def doc_positions(doc_ids):
@@ -116,29 +133,23 @@
     queries = rotate(projected[:, :query_cols].reshape(micro_rows, heads_here, HD), places)
     key_heads, value_heads = split_pairs(projected[:, query_cols:], places)
     mixed = attend(queries, key_heads, value_heads, doc_ids)
-    total = lax.psum_scatter(
-        jnp.dot(mixed, out_local, preferred_element_type=jnp.float32).astype(jnp.bfloat16),
-        "tensor",
-        scatter_dimension=0,
-        tiled=True,
-    ).astype(jnp.float32)
+    total = scatter_sum(mixed, out_local)
     halfway = current + total
     hidden = expand(
         lax.all_gather(normalize(halfway, gain_forward), "tensor", axis=0, tiled=True),
         gate_local,
         up_local,
     )
-    forward = lax.psum_scatter(
-        jnp.dot(hidden, down_local, preferred_element_type=jnp.float32).astype(jnp.bfloat16),
-        "tensor",
-        scatter_dimension=0,
-        tiled=True,
-    ).astype(jnp.float32)
+    forward = scatter_sum(hidden, down_local)
     return halfway + forward
 
 
-def pass_on(result):
-    return shifted(result.astype(jnp.bfloat16), "pipe", 1).astype(result.dtype)
+def pass_on(result, moment, micro_count):
+    last = lax.axis_size("pipe") - 1
+    pairs = [(i, i + 1) for i in range(last) if 0 <= moment - i < micro_count]
+    if moment >= last:
+        pairs.append((last, moment - last))
+    return lax.ppermute(result.astype(jnp.bfloat16), "pipe", pairs).astype(jnp.float32)
 
 
 def shards(
@@ -208,7 +219,7 @@
     )
     phase_index = lax.axis_index("pipe")
     carried = jnp.zeros((slab_rows, width), jnp.float32)
-    finished = []
+    out = jnp.zeros((slab_rows, width), jnp.float32)
     for moment in range(micro_count + pipe_count - 1):
         feed_rows = micro_batches[min(moment, micro_count - 1)].astype(jnp.float32)
         current = jnp.where(
@@ -217,14 +228,14 @@
         micro_index = jnp.clip(moment - phase_index, 0, micro_count - 1)
         doc_ids = lax.dynamic_index_in_dim(segments, micro_index, 0, keepdims=False)
         result = run_layer(current, doc_ids, layer_weights)
-        if moment >= pipe_count - 1:
-            finished.append(result)
+        home = moment - (pipe_count - 1)
         if moment < micro_count + pipe_count - 2:
-            carried = pass_on(result)
-    everyone = broadcast(jnp.stack(finished).astype(jnp.bfloat16), "pipe", pipe_count - 1).astype(
-        jnp.float32
-    )
-    return lax.dynamic_index_in_dim(everyone, phase_index, 0, keepdims=False)
+            carried = pass_on(result, moment, micro_count)
+            if home >= 0:
+                out = jnp.where(phase_index == home, carried, out)
+        else:
+            out = jnp.where(phase_index == home, result, out)
+    return out
 
 
 def solution(mesh):

time: 1280 us -> 679 us (0.53)
  waiting for transfers between devices: 801 us -> 142 us
  blocking collectives: 292 us -> 381 us
  matrix products: 95.4 us -> 34.8 us
  starting transfers between devices: 18.5 us -> 63.3 us
    reduce_scatter x14 -> x0, waiting for transfers between devices: 722 us -> none  [the longest x7 363 us: run_layer(): lax.psum_scatter(jnp.dot(mixed, out_local, preferred_element_type=jnp.flo...]
    all_to_all x0 -> x7, blocking collectives: none -> 129 us  [scatter_sum(): lax.all_to_all(pair.reshape(chips, rows, -1), 'tensor', split_axis=0, con...]
    all_to_all x0 -> x7, waiting for transfers between devices: none -> 92.3 us  [scatter_sum(): lax.all_to_all(pair.reshape(chips, rows, -1), 'tensor', split_axis=0, con...]
    psum x1 -> x0, waiting for transfers between devices: 44.9 us -> none  [broadcast(): return lax.psum(block, axis)]
    dot_general x14 -> x28, matrix products: 47.1 us -> 12.2 us  [the longest x14 6.55 us: scatter_sum(): part = jnp.dot(ordered, weight, preferred_element_type=jnp.float32)]
    all_to_all x0 -> x7, starting transfers between devices: none -> 28.4 us  [scatter_sum(): lax.all_to_all(pair.reshape(chips, rows, -1), 'tensor', split_axis=0, con...]
    ppermute x7 -> x21, waiting for transfers between devices: 7.33 us -> 29.2 us  [swapped(): return lax.ppermute(value, axis, pairs)]
    all_gather x7, blocking collectives: 152 us -> 131 us  [run_layer(): lax.all_gather(normalize(current, gain_attention), 'tensor', axis=0, tile...]
  transfers between devices with their start and end apart: 30 -> 36, of which waited for: 29 -> 33; matrix products, arithmetic and copies ran while one was open for 1% -> 3% of each run, Pallas kernels for 0% -> 0%
where the time goes in v1:
time: 679 us; the launch traced here: 673 us
  blocking collectives  381 us (56%)
  waiting for transfers between devices  142 us (21%)
  starting transfers between devices  63.3 us (9%)
  other arithmetic  38.1 us (6%)
  matrix products  34.8 us (5%)
  local copies, waits for them, and re-layouts  11.8 us (2%)
    all_gather x7, blocking collectives, run_layer(): lax.all_gather(normalize(current, gain_attention), 'tensor', axis=0, tile...  131 us
    all_to_all x7, blocking collectives, scatter_sum(): lax.all_to_all(pair.reshape(chips, rows, -1), 'tensor', split_axis=0, con...  129 us
    all_gather x7, blocking collectives, run_layer(): lax.all_gather(normalize(halfway, gain_forward), 'tensor', axis=0, tiled=...  121 us
    all_to_all x7, waiting for transfers between devices, scatter_sum(): lax.all_to_all(pair.reshape(chips, rows, -1), 'tensor', split_axis=0, con...  92.3 us
    ppermute x21, waiting for transfers between devices, swapped(): return lax.ppermute(value, axis, pairs)  29.2 us
    all_to_all x7, starting transfers between devices, scatter_sum(): lax.all_to_all(pair.reshape(chips, rows, -1), 'tensor', split_axis=0, con...  28.4 us
    ppermute x6, waiting for transfers between devices, pass_on(): lax.ppermute(result.astype(jnp.bfloat16), 'pipe', pairs).astype(jnp.float32)  16.3 us
    ppermute x21, starting transfers between devices, swapped(): return lax.ppermute(value, axis, pairs)  14.2 us
  transfers between devices with their start and end apart: 36, of which 33 were waited for; matrix products, arithmetic and copies ran while one was open for 3% of the time, Pallas kernels for 0%

profile of v1, /device:TPU:7, one launch (start us, length us, event | category | flops | bytes accessed | tf_op | source)
XLA Modules:
  0.0 672.8 jit_solution(16124467686262850466)
XLA Ops:
  25.9 24.7 %all_gather.42 = bf16[128,3072]{1,0:T(8,128)(2,1)S(1)} all-gather(bf16[8,3072]{1,0:T(8,128)(2,1)S(1)} %multiply_convert_fusion.10), channel_id=1, replica_groups=mesh['dp'=4,'pipe'=4,'tensor'=16] {'tensor'}, dimensions={0}, use_global_device_ids=true | all-gather | bytes 835584 | tf_op jit(solution)/shard_map/all_gather | solution.py:124
  58.2 18.5 %all_to_all.84 = bf16[8,8,3072]{2,1,0:T(8,128)(2,1)S(1)} all-to-all(bf16[8,8,3072]{2,1,0:T(8,128)(2,1)S(1)} %fusion.147), channel_id=1, replica_groups={{0,2,4,6,8,10,12,14},{1,3,5,7,9,11,13,15},{16,18,20,22,24,26,28,30},{17..., dimensions={0} | all-to-all | bytes 786432 | tf_op jit(solution)/shard_map/all_to_all | solution.py:32
  77.0 17.2 %all_gather.43 = bf16[128,3072]{1,0:T(8,128)(2,1)S(1)} all-gather(bf16[8,3072]{1,0:T(8,128)(2,1)S(1)} %multiply_convert_fusion.9), channel_id=1, replica_groups=mesh['dp'=4,'pipe'=4,'tensor'=16] {'tensor'}, dimensions={0}, use_global_device_ids=true | all-gather | bytes 835584 | tf_op jit(solution)/shard_map/all_gather | solution.py:139
  120.3 17.1 %all_gather.44 = bf16[128,3072]{1,0:T(8,128)(2,1)S(1)} all-gather(bf16[8,3072]{1,0:T(8,128)(2,1)S(1)} %multiply_convert_fusion.8), channel_id=1, replica_groups=mesh['dp'=4,'pipe'=4,'tensor'=16] {'tensor'}, dimensions={0}, use_global_device_ids=true | all-gather | bytes 835584 | tf_op jit(solution)/shard_map/all_gather | solution.py:124
  143.9 18.2 %all_to_all.85 = bf16[8,8,3072]{2,1,0:T(8,128)(2,1)S(1)} all-to-all(bf16[8,8,3072]{2,1,0:T(8,128)(2,1)S(1)} %fusion.149), channel_id=1, replica_groups={{0,2,4,6,8,10,12,14},{1,3,5,7,9,11,13,15},{16,18,20,22,24,26,28,30},{17..., dimensions={0} | all-to-all | bytes 786432 | tf_op jit(solution)/shard_map/all_to_all | solution.py:32
  162.4 17.6 %all_gather.45 = bf16[128,3072]{1,0:T(8,128)(2,1)S(1)} all-gather(bf16[8,3072]{1,0:T(8,128)(2,1)S(1)} %multiply_convert_fusion.7), channel_id=1, replica_groups=mesh['dp'=4,'pipe'=4,'tensor'=16] {'tensor'}, dimensions={0}, use_global_device_ids=true | all-gather | bytes 835584 | tf_op jit(solution)/shard_map/all_gather | solution.py:139
  206.0 17.1 %all_gather.46 = bf16[128,3072]{1,0:T(8,128)(2,1)S(1)} all-gather(bf16[8,3072]{1,0:T(8,128)(2,1)S(1)} %multiply_convert_fusion.6), channel_id=1, replica_groups=mesh['dp'=4,'pipe'=4,'tensor'=16] {'tensor'}, dimensions={0}, use_global_device_ids=true | all-gather | bytes 835584 | tf_op jit(solution)/shard_map/all_gather | solution.py:124
  230.3 18.2 %all_to_all.86 = bf16[8,8,3072]{2,1,0:T(8,128)(2,1)S(1)} all-to-all(bf16[8,8,3072]{2,1,0:T(8,128)(2,1)S(1)} %fusion.151), channel_id=1, replica_groups={{0,2,4,6,8,10,12,14},{1,3,5,7,9,11,13,15},{16,18,20,22,24,26,28,30},{17..., dimensions={0} | all-to-all | bytes 786432 | tf_op jit(solution)/shard_map/all_to_all | solution.py:32
  248.9 17.4 %all_gather.47 = bf16[128,3072]{1,0:T(8,128)(2,1)S(1)} all-gather(bf16[8,3072]{1,0:T(8,128)(2,1)S(1)} %multiply_convert_fusion.5), channel_id=1, replica_groups=mesh['dp'=4,'pipe'=4,'tensor'=16] {'tensor'}, dimensions={0}, use_global_device_ids=true | all-gather | bytes 835584 | tf_op jit(solution)/shard_map/all_gather | solution.py:139
  304.5 18.0 %all_gather.48 = bf16[128,3072]{1,0:T(8,128)(2,1)S(1)} all-gather(bf16[8,3072]{1,0:T(8,128)(2,1)S(1)} %multiply_convert_fusion.4), channel_id=1, replica_groups=mesh['dp'=4,'pipe'=4,'tensor'=16] {'tensor'}, dimensions={0}, use_global_device_ids=true | all-gather | bytes 835584 | tf_op jit(solution)/shard_map/all_gather | solution.py:124
  337.7 18.2 %all_to_all.87 = bf16[8,8,3072]{2,1,0:T(8,128)(2,1)S(1)} all-to-all(bf16[8,8,3072]{2,1,0:T(8,128)(2,1)S(1)} %fusion.153), channel_id=1, replica_groups={{0,2,4,6,8,10,12,14},{1,3,5,7,9,11,13,15},{16,18,20,22,24,26,28,30},{17..., dimensions={0} | all-to-all | bytes 786432 | tf_op jit(solution)/shard_map/all_to_all | solution.py:32
  356.9 17.4 %all_gather.49 = bf16[128,3072]{1,0:T(8,128)(2,1)S(1)} all-gather(bf16[8,3072]{1,0:T(8,128)(2,1)S(1)} %multiply_convert_fusion.3), channel_id=1, replica_groups=mesh['dp'=4,'pipe'=4,'tensor'=16] {'tensor'}, dimensions={0}, use_global_device_ids=true | all-gather | bytes 835584 | tf_op jit(solution)/shard_map/all_gather | solution.py:139
  402.0 18.0 %all_gather.50 = bf16[128,3072]{1,0:T(8,128)(2,1)S(1)} all-gather(bf16[8,3072]{1,0:T(8,128)(2,1)S(1)} %fusion.179), channel_id=1, replica_groups=mesh['dp'=4,'pipe'=4,'tensor'=16] {'tensor'}, dimensions={0}, use_global_device_ids=true | all-gather | bytes 835584 | tf_op jit(solution)/shard_map/all_gather | solution.py:124
  427.2 18.5 %all_to_all.88 = bf16[8,8,3072]{2,1,0:T(8,128)(2,1)S(1)} all-to-all(bf16[8,8,3072]{2,1,0:T(8,128)(2,1)S(1)} %fusion.155), channel_id=1, replica_groups={{0,2,4,6,8,10,12,14},{1,3,5,7,9,11,13,15},{16,18,20,22,24,26,28,30},{17..., dimensions={0} | all-to-all | bytes 786432 | tf_op jit(solution)/shard_map/all_to_all | solution.py:32
  446.0 17.2 %all_gather.51 = bf16[128,3072]{1,0:T(8,128)(2,1)S(1)} all-gather(bf16[8,3072]{1,0:T(8,128)(2,1)S(1)} %multiply_convert_fusion.2), channel_id=1, replica_groups=mesh['dp'=4,'pipe'=4,'tensor'=16] {'tensor'}, dimensions={0}, use_global_device_ids=true | all-gather | bytes 835584 | tf_op jit(solution)/shard_map/all_gather | solution.py:139
  472.4 14.8 %all-to-all-done.11 = bf16[8,8,3072]{2,1,0:T(8,128)(2,1)} async-done(((bf16[8,8,3072]{2,1,0:T(8,128)(2,1)}), bf16[8,8,3072]{2,1,0:T(8,128)(2,1)}, u32[]{:S(2)}, u32[]{:S(2)}) %all-to-all-start.11) | async-done | bytes 393248 | tf_op jit(solution)/shard_map/all_to_all | solution.py:32
  495.5 18.0 %all_gather.52 = bf16[128,3072]{1,0:T(8,128)(2,1)S(1)} all-gather(bf16[8,3072]{1,0:T(8,128)(2,1)S(1)} %fusion.182), channel_id=1, replica_groups=mesh['dp'=4,'pipe'=4,'tensor'=16] {'tensor'}, dimensions={0}, use_global_device_ids=true | all-gather | bytes 835584 | tf_op jit(solution)/shard_map/all_gather | solution.py:124
  520.1 18.5 %all_to_all.89 = bf16[8,8,3072]{2,1,0:T(8,128)(2,1)S(1)} all-to-all(bf16[8,8,3072]{2,1,0:T(8,128)(2,1)S(1)} %fusion.157), channel_id=1, replica_groups={{0,2,4,6,8,10,12,14},{1,3,5,7,9,11,13,15},{16,18,20,22,24,26,28,30},{17..., dimensions={0} | all-to-all | bytes 786432 | tf_op jit(solution)/shard_map/all_to_all | solution.py:32
  538.9 17.2 %all_gather.53 = bf16[128,3072]{1,0:T(8,128)(2,1)S(1)} all-gather(bf16[8,3072]{1,0:T(8,128)(2,1)S(1)} %multiply_convert_fusion.1), channel_id=1, replica_groups=mesh['dp'=4,'pipe'=4,'tensor'=16] {'tensor'}, dimensions={0}, use_global_device_ids=true | all-gather | bytes 835584 | tf_op jit(solution)/shard_map/all_gather | solution.py:139
  565.3 14.6 %all-to-all-done.13 = bf16[8,8,3072]{2,1,0:T(8,128)(2,1)} async-done(((bf16[8,8,3072]{2,1,0:T(8,128)(2,1)}), bf16[8,8,3072]{2,1,0:T(8,128)(2,1)}, u32[]{:S(2)}, u32[]{:S(2)}) %all-to-all-start.13) | async-done | bytes 393248 | tf_op jit(solution)/shard_map/all_to_all | solution.py:32
  586.2 18.3 %all_gather.54 = bf16[128,3072]{1,0:T(8,128)(2,1)S(1)} all-gather(bf16[8,3072]{1,0:T(8,128)(2,1)S(1)} %fusion.185), channel_id=1, replica_groups=mesh['dp'=4,'pipe'=4,'tensor'=16] {'tensor'}, dimensions={0}, use_global_device_ids=true | all-gather | bytes 835584 | tf_op jit(solution)/shard_map/all_gather | solution.py:124
  611.0 18.5 %all_to_all.90 = bf16[8,8,3072]{2,1,0:T(8,128)(2,1)S(1)} all-to-all(bf16[8,8,3072]{2,1,0:T(8,128)(2,1)S(1)} %fusion.159), channel_id=1, replica_groups={{0,2,4,6,8,10,12,14},{1,3,5,7,9,11,13,15},{16,18,20,22,24,26,28,30},{17..., dimensions={0} | all-to-all | bytes 786432 | tf_op jit(solution)/shard_map/all_to_all | solution.py:32
  629.8 17.2 %all_gather.55 = bf16[128,3072]{1,0:T(8,128)(2,1)S(1)} all-gather(bf16[8,3072]{1,0:T(8,128)(2,1)S(1)} %multiply_convert_fusion), channel_id=1, replica_groups=mesh['dp'=4,'pipe'=4,'tensor'=16] {'tensor'}, dimensions={0}, use_global_device_ids=true | all-gather | bytes 835584 | tf_op jit(solution)/shard_map/all_gather | solution.py:139
  655.6 15.2 %all-to-all-done.15 = bf16[8,8,3072]{2,1,0:T(8,128)(2,1)} async-done(((bf16[8,8,3072]{2,1,0:T(8,128)(2,1)}), bf16[8,8,3072]{2,1,0:T(8,128)(2,1)}, u32[]{:S(2)}, u32[]{:S(2)}) %all-to-all-start.15) | async-done | bytes 393248 | tf_op jit(solution)/shard_map/all_to_all | solution.py:32
  (393 shorter events, 245.0 us)
Async XLA Ops:
  2.5 9.4 %all-to-all-start = ((s32[4,1,16]{2,1,0:T(1,128)}), s32[4,1,16]{2,1,0:T(1,128)S(1)}, u32[]{:S(2)}, u32[]{:S(2)}) async-start(s32[4,1,16]{2,1,0:T(1,128)} %bitcast), calls=%async_computation | async-start | bytes 4096 | tf_op jit(solution)/shard_map/all_to_all | solution.py:196
  11.9 10.5 %all-to-all-start.1 = ((bf16[4,16,3072]{2,1,0:T(8,128)(2,1)}), bf16[4,16,3072]{2,1,0:T(8,128)(2,1)S(1)}, u32[]{:S(2)}, u32[]{:S(2)}) async-start(bf16[4,16,3072]{2,1,0:T(8,128)(2,1)} %bitcast.2), calls=%async_computation.1 | async-start | bytes 786432 | tf_op jit(solution)/shard_map/all_to_all | solution.py:189
  56.3 1.8 collective-permute-start.1
  96.1 1.8 collective-permute-start.2
  98.8 19.4 %all-to-all-start.3 = ((bf16[8,8,3072]{2,1,0:T(8,128)(2,1)}), bf16[8,8,3072]{2,1,0:T(8,128)(2,1)}, u32[]{:S(2)}, u32[]{:S(2)}) async-start(bf16[8,8,3072]{2,1,0:T(8,128)(2,1)} %fusion.148), calls=%async_computation.3 | async-start | bytes 786432 | tf_op jit(solution)/shard_map/all_to_all | solution.py:32
  142.0 1.8 collective-permute-start.5
  182.0 1.8 collective-permute-start.6
  184.6 19.3 %all-to-all-start.5 = ((bf16[8,8,3072]{2,1,0:T(8,128)(2,1)}), bf16[8,8,3072]{2,1,0:T(8,128)(2,1)}, u32[]{:S(2)}, u32[]{:S(2)}) async-start(bf16[8,8,3072]{2,1,0:T(8,128)(2,1)} %fusion.150), calls=%async_computation.5 | async-start | bytes 786432 | tf_op jit(solution)/shard_map/all_to_all | solution.py:32
  228.5 1.8 collective-permute-start.9
  268.1 1.8 collective-permute-start.10
  270.8 19.3 %all-to-all-start.7 = ((bf16[8,8,3072]{2,1,0:T(8,128)(2,1)}), bf16[8,8,3072]{2,1,0:T(8,128)(2,1)}, u32[]{:S(2)}, u32[]{:S(2)}) async-start(bf16[8,8,3072]{2,1,0:T(8,128)(2,1)} %fusion.152), calls=%async_computation.7 | async-start | bytes 786432 | tf_op jit(solution)/shard_map/all_to_all | solution.py:32
  291.2 13.0 %collective-permute-start.11 = (bf16[8,3072]{1,0:T(8,128)(2,1)S(1)}, bf16[8,3072]{1,0:T(8,128)(2,1)S(1)}, u32[]{:S(2)}, u32[]{:S(2)}) collective-permute-start(bf16[8,3072]{1,0:T(8,128)(2,1)S(1)} %add_convert_fusion.3), channel_id=1, source_target_pairs={{0,16},{16,32},{32,48},{1,17},{17,33},{33,49},{2,18},{18,34},{34,5... | collective-permute-start | bytes 147464 | tf_op jit(solution)/shard_map/ppermute | solution.py:152
  327.1 10.6 %collective-permute-start.13 = (bf16[64,3072]{1,0:T(8,128)(2,1)S(1)}, bf16[64,3072]{1,0:T(8,128)(2,1)S(1)}, u32[]{:S(2)}, u32[]{:S(2)}) collective-permute-start(bf16[64,3072]{1,0:T(8,128)(2,1)S(1)} %slice.866), channel_id=1, source_target_pairs={{0,1},{1,0},{2,3},{3,2},{4,5},{5,4},{6,7},{7,6},{8,9},{9,8},{10,11... | collective-permute-start | bytes 1179656 | tf_op jit(solution)/shard_map/ppermute | solution.py:12
  376.1 1.8 collective-permute-start.14
  378.7 18.7 %all-to-all-start.9 = ((bf16[8,8,3072]{2,1,0:T(8,128)(2,1)}), bf16[8,8,3072]{2,1,0:T(8,128)(2,1)S(1)}, u32[]{:S(2)}, u32[]{:S(2)}) async-start(bf16[8,8,3072]{2,1,0:T(8,128)(2,1)} %fusion.154), calls=%async_computation.9 | async-start | bytes 786432 | tf_op jit(solution)/shard_map/all_to_all | solution.py:32
  398.5 3.3 collective-permute-start.15
  425.3 1.8 collective-permute-start.17
  465.1 1.8 collective-permute-start.18
  467.7 19.4 %all-to-all-start.11 = ((bf16[8,8,3072]{2,1,0:T(8,128)(2,1)}), bf16[8,8,3072]{2,1,0:T(8,128)(2,1)}, u32[]{:S(2)}, u32[]{:S(2)}) async-start(bf16[8,8,3072]{2,1,0:T(8,128)(2,1)} %fusion.156), calls=%async_computation.11 | async-start | bytes 786432 | tf_op jit(solution)/shard_map/all_to_all | solution.py:32
  488.4 6.9 %collective-permute-start.19 = (bf16[8,3072]{1,0:T(8,128)(2,1)S(1)}, bf16[8,3072]{1,0:T(8,128)(2,1)S(1)}, u32[]{:S(2)}, u32[]{:S(2)}) collective-permute-start(bf16[8,3072]{1,0:T(8,128)(2,1)S(1)} %add_convert_fusion.1), channel_id=1, source_target_pairs={{16,32},{32,48},{48,16},{17,33},{33,49},{49,17},{18,34},{34,50},{5... | collective-permute-start | bytes 147464 | tf_op jit(solution)/shard_map/ppermute | solution.py:152
  518.2 1.8 collective-permute-start.21
  560.7 19.3 %all-to-all-start.13 = ((bf16[8,8,3072]{2,1,0:T(8,128)(2,1)}), bf16[8,8,3072]{2,1,0:T(8,128)(2,1)}, u32[]{:S(2)}, u32[]{:S(2)}) async-start(bf16[8,8,3072]{2,1,0:T(8,128)(2,1)} %fusion.158), calls=%async_computation.13 | async-start | bytes 786432 | tf_op jit(solution)/shard_map/all_to_all | solution.py:32
  581.2 4.8 collective-permute-start.23
  651.5 19.3 %all-to-all-start.15 = ((bf16[8,8,3072]{2,1,0:T(8,128)(2,1)}), bf16[8,8,3072]{2,1,0:T(8,128)(2,1)}, u32[]{:S(2)}, u32[]{:S(2)}) async-start(bf16[8,8,3072]{2,1,0:T(8,128)(2,1)} %fusion.160), calls=%async_computation.15 | async-start | bytes 786432 | tf_op jit(solution)/shard_map/all_to_all | solution.py:32
  (55 other events, 1188.7 us)

commit v2 on v1

v2 whole, which is shorter than its diff:
```python
import jax
import jax.numpy as jnp
from jax import lax
from jax.experimental import pallas as pl
from jax.experimental.pallas import tpu as pltpu
from jax.sharding import PartitionSpec as P

HD = 128
CORES = 2
VMEM_LIMIT = 52 * 2**20


def swapped(value):
    pairs = [(source, source ^ 1) for source in range(lax.axis_size("tensor"))]
    return lax.ppermute(value, "tensor", pairs)


def parity():
    return lax.axis_index("tensor") % CORES


def scatter_sum(left, weight):
    peers = lax.axis_size("tensor")
    chips = peers // CORES
    rows = left.shape[0] // peers
    split = left.reshape(chips, CORES, rows, -1)
    mine = jnp.where(parity() == 0, split[:, 0], split[:, 1])
    other = jnp.where(parity() == 0, split[:, 1], split[:, 0])
    ordered = jnp.concatenate([other, mine], axis=0).reshape(left.shape)
    part = jnp.dot(ordered, weight, preferred_element_type=jnp.float32)
    half = chips * rows
    got = swapped(part[:half].astype(jnp.bfloat16))
    pair = (part[half:] + got.astype(jnp.float32)).astype(jnp.bfloat16)
    blocks = lax.all_to_all(
        pair.reshape(chips, rows, -1),
        "tensor",
        split_axis=0,
        concat_axis=0,
        tiled=True,
        axis_index_groups=[list(range(core, peers, CORES)) for core in range(CORES)],
    )
    return jnp.sum(blocks.astype(jnp.float32), axis=0)


def tables(doc_ids):
    order = jnp.arange(doc_ids.shape[1], dtype=jnp.int32)
    same = doc_ids[:, :, None] == doc_ids[:, None, :]
    seen = jnp.logical_and(same, order[None, :] <= order[:, None])
    places = jnp.sum(seen.astype(jnp.float32), axis=-1) - 1.0
    half = HD // 2
    frequency = 500000.0 ** (-(jnp.arange(half, dtype=jnp.float32) * 2.0 / HD))
    angles = places[:, :, None] * frequency
    cosine, sine = jnp.cos(angles), jnp.sin(angles)
    return (
        jnp.concatenate([cosine, cosine], axis=-1),
        jnp.concatenate([-sine, sine], axis=-1),
        seen.astype(jnp.float32),
    )


def normalize(rows_in, gain):
    meansq = jnp.mean(rows_in * rows_in, axis=-1, keepdims=True)
    return (rows_in * lax.rsqrt(meansq + 1e-05) * gain).astype(jnp.bfloat16)


def split_float(values):
    high = values.astype(jnp.bfloat16)
    return high, (values - high.astype(jnp.float32)).astype(jnp.bfloat16)


def attend(queries, keys, values, seen):
    query_high, query_low = split_float(queries)
    key_high, key_low = split_float(keys)
    scores = lax.dot_general(
        jnp.concatenate([query_high, query_high, query_low], axis=1),
        jnp.concatenate([key_high, key_low, key_high], axis=1),
        (((1,), (1,)), ((), ())),
        preferred_element_type=jnp.float32,
    ) * HD ** (-0.5)
    scores = jnp.where(seen > 0.5, scores, jnp.float32(-1e30))
    spread = jnp.exp(scores - jnp.max(scores, axis=-1, keepdims=True))
    weights = (spread / jnp.sum(spread, axis=-1, keepdims=True)).astype(jnp.bfloat16)
    return jnp.dot(weights, values, preferred_element_type=jnp.float32).astype(jnp.bfloat16)


def attend_local(piece, query_local, pair_local, turns):
    cosine, sine, seen = turns

    def turn(head):
        front, back = head[:, : HD // 2], head[:, HD // 2 :]
        return head * cosine + jnp.concatenate([back, front], axis=1) * sine

    queries = turn(jnp.dot(piece, query_local, preferred_element_type=jnp.float32))
    pair = jnp.dot(piece, pair_local, preferred_element_type=jnp.float32)
    mine = jnp.where(parity() == 0, turn(pair), pair)
    partner = swapped(mine.astype(jnp.bfloat16)).astype(mine.dtype)
    keys = jnp.where(parity() == 0, mine, partner)
    values = jnp.where(parity() == 0, partner, mine).astype(jnp.bfloat16)
    return attend(queries, keys, values, seen)


def whole_projections(query_local, pair_local):
    both = jnp.concatenate([query_local, pair_local], axis=1)
    half = both.shape[0] // 2
    first, second = both[:half], both[half:]
    kept = jnp.where(parity() == 0, first, second)
    got = swapped(jnp.where(parity() == 0, second, first))
    block = jnp.where(
        parity() == 0,
        jnp.concatenate([kept, got], axis=1),
        jnp.concatenate([got, kept], axis=1),
    )
    whole = lax.all_gather(block, "tensor", axis=0, tiled=True)
    return whole.reshape(-1, 2 * half, block.shape[1])


def attention_body(
    where_ref,
    x_ref,
    gain_ref,
    cosine_ref,
    sine_ref,
    seen_ref,
    in_hbm,
    out_hbm,
    total_ref,
    normed_ref,
    in_ref,
    out_ref,
    in_sem,
    out_sem,
):
    groups = in_ref.shape[0]
    rows, width = x_ref.shape
    inner = out_hbm.shape[2]
    strip = 16
    micro, core = where_ref[0], where_ref[1]
    fetch_in = [
        pltpu.make_async_copy(in_hbm.at[group, core], in_ref.at[group], in_sem.at[group])
        for group in range(groups)
    ]
    fetch_out = [
        pltpu.make_async_copy(
            out_hbm.at[group, core],
            out_ref.at[pl.ds(group * inner, inner), :],
            out_sem.at[group],
        )
        for group in range(groups)
    ]
    for copy in fetch_in + fetch_out:
        copy.start()

    @pl.loop(0, rows // strip)
    def _(index):
        part = pl.ds(pl.multiple_of(index * strip, strip), strip)
        normed_ref[part, :] = normalize(x_ref[part, :].astype(jnp.float32), gain_ref[...])

    cosine, sine, seen = cosine_ref[micro], sine_ref[micro], seen_ref[micro]
    seen_twice = jnp.concatenate([seen, seen], axis=0)

    def turn(head):
        return head * cosine + pltpu.roll(head, HD // 2, 1) * sine

    def project(group):
        fetch_in[group].wait()
        return jnp.dot(normed_ref[...], in_ref[group], preferred_element_type=jnp.float32)

    mixed = []
    heads = project(0)
    for group in range(groups):
        later = project(group + 1) if group + 1 < groups else None
        queries = jnp.concatenate(
            [turn(heads[:, :HD]), turn(heads[:, 2 * HD : 3 * HD])], axis=0
        )
        both = attend(
            queries,
            turn(heads[:, HD : 2 * HD]),
            heads[:, 3 * HD :].astype(jnp.bfloat16),
            seen_twice,
        )
        mixed += [both[:rows], both[rows:]]
        heads = later
    left = jnp.concatenate(mixed, axis=1)
    for copy in fetch_out:
        copy.wait()
    tile = 512

    @pl.loop(0, width // tile)
    def _(index):
        part = pl.ds(pl.multiple_of(index * tile, tile), tile)
        total_ref[:, part] = jnp.dot(
            left, out_ref[:, part], preferred_element_type=jnp.float32
        ).astype(jnp.bfloat16)


def attention_half(everyone, micro_index, turns, whole_in, whole_out, gain):
    rows, width = everyone.shape
    chips, _, columns = whole_in.shape
    groups = chips // CORES
    inner = whole_out.shape[0] // chips
    vmem = pl.BlockSpec(memory_space=pltpu.VMEM)
    hbm = pl.BlockSpec(memory_space=pltpu.HBM)
    return pl.pallas_call(
        attention_body,
        in_specs=[pl.BlockSpec(memory_space=pltpu.SMEM)] + [vmem] * 5 + [hbm] * 2,
        out_specs=vmem,
        scratch_shapes=[
            pltpu.VMEM((rows, width), jnp.bfloat16),
            pltpu.VMEM((groups, width, columns), jnp.bfloat16),
            pltpu.VMEM((groups * inner, width), jnp.bfloat16),
            pltpu.SemaphoreType.DMA((groups,)),
            pltpu.SemaphoreType.DMA((groups,)),
        ],
        out_shape=jax.ShapeDtypeStruct((rows, width), jnp.bfloat16),
        compiler_params=pltpu.CompilerParams(vmem_limit_bytes=VMEM_LIMIT),
        cost_estimate=pl.CostEstimate(
            flops=2 * rows * width * groups * (columns + inner),
            bytes_accessed=2 * width * groups * (columns + inner),
            transcendentals=2 * rows * rows * groups,
        ),
    )(
        jnp.stack([micro_index, parity()]).astype(jnp.int32),
        everyone,
        gain[None],
        *turns,
        whole_in.reshape(groups, CORES, width, columns),
        whole_out.reshape(groups, CORES, inner, width),
    )


def run_layer(current, micro_index, turns, layer_weights, whole_in, whole_out):
    (
        query_local,
        pair_local,
        out_local,
        gate_local,
        up_local,
        down_local,
        gain_attention,
        gain_forward,
    ) = layer_weights
    slab_rows = current.shape[0]
    everyone = lax.all_gather(current, "tensor", axis=0, tiled=True)
    if whole_in is not None:
        part = attention_half(everyone, micro_index, turns, whole_in, whole_out, gain_attention)
        total = part.astype(jnp.float32) + swapped(part).astype(jnp.float32)
    else:
        now = [lax.dynamic_index_in_dim(table, micro_index, 0, keepdims=False) for table in turns]
        piece = normalize(everyone.astype(jnp.float32), gain_attention)
        mixed = attend_local(piece, query_local, pair_local, now)
        if whole_out is not None:
            heads = lax.all_gather(mixed, "tensor", axis=1, tiled=True)
            total = jnp.dot(heads, whole_out, preferred_element_type=jnp.float32)
    if whole_out is not None:
        halfway_all = everyone.astype(jnp.float32) + total
        piece = normalize(halfway_all, gain_forward)
        start = lax.axis_index("tensor") * slab_rows
        halfway = lax.dynamic_slice_in_dim(halfway_all, start, slab_rows, 0)
    else:
        halfway = current.astype(jnp.float32) + scatter_sum(mixed, out_local)
        piece = lax.all_gather(normalize(halfway, gain_forward), "tensor", axis=0, tiled=True)
    gate = jnp.dot(piece, gate_local, preferred_element_type=jnp.float32)
    upward = jnp.dot(piece, up_local, preferred_element_type=jnp.float32)
    hidden = (jax.nn.silu(gate) * upward).astype(jnp.bfloat16)
    return halfway + scatter_sum(hidden, down_local)


def pass_on(result, moment, micro_count):
    last = lax.axis_size("pipe") - 1
    pairs = [(i, i + 1) for i in range(last) if 0 <= moment - i < micro_count]
    if moment >= last:
        pairs.append((last, moment - last))
    return lax.ppermute(result.astype(jnp.bfloat16), "pipe", pairs)


def regroup(tokens, destination, group_count, group_span, micro_rows, slab_rows):
    held_rows, width = tokens.shape
    capacity = held_rows // 2
    slots = group_count * capacity
    target = destination // group_span
    within = destination % group_span
    landing = within // micro_rows * slab_rows + within % slab_rows
    order = jnp.arange(held_rows, dtype=jnp.int32)
    ahead = jnp.logical_and(target[:, None] == target[None, :], order[None, :] < order[:, None])
    slot_index = target * capacity + jnp.sum(ahead.astype(jnp.int32), axis=1)
    to_slot = jnp.arange(slots, dtype=jnp.int32)[:, None] == slot_index[None, :]
    mark = jnp.broadcast_to((landing + 1).astype(jnp.bfloat16)[:, None], (held_rows, HD))
    sent = jnp.dot(
        to_slot.astype(jnp.bfloat16),
        jnp.concatenate([tokens, mark], axis=1),
        preferred_element_type=jnp.float32,
    ).astype(jnp.bfloat16)
    got = lax.all_to_all(
        sent.reshape(group_count, capacity, width + HD),
        "dp",
        split_axis=0,
        concat_axis=0,
        tiled=True,
    ).reshape(slots, width + HD)
    place = got[:, width].astype(jnp.int32) - 1
    to_row = order[:, None] == place[None, :]
    return jnp.dot(
        to_row.astype(jnp.bfloat16), got[:, :width], preferred_element_type=jnp.float32
    ).astype(jnp.bfloat16)


def shards(
    tokens,
    destination,
    segments,
    query_weight,
    key_value_weight,
    out_weight,
    gate_weight,
    up_weight,
    down_weight,
    attention_gain,
    forward_gain,
):
    pipe_count = lax.axis_size("pipe")
    micro_count, micro_rows = segments.shape
    slab_rows = micro_rows // lax.axis_size("tensor")
    width = tokens.shape[1]
    whole_out = lax.all_gather(out_weight[0], "tensor", axis=0, tiled=True)
    whole_in = whole_projections(query_weight[0], key_value_weight[0])
    regrouped = regroup(
        tokens,
        destination,
        lax.axis_size("dp"),
        micro_count * micro_rows,
        micro_rows,
        slab_rows,
    )
    micro_batches = regrouped.reshape(micro_count, slab_rows, width)
    turns = tables(segments)
    layer_weights = (
        query_weight[0],
        key_value_weight[0],
        out_weight[0],
        gate_weight[0],
        up_weight[0],
        down_weight[0],
        attention_gain[0],
        forward_gain[0],
    )
    phase_index = lax.axis_index("pipe")
    carried = jnp.zeros((slab_rows, width), jnp.bfloat16)
    out = jnp.zeros((slab_rows, width), jnp.float32)
    for moment in range(micro_count + pipe_count - 1):
        current = carried
        if moment < micro_count:
            current = jnp.where(phase_index == 0, micro_batches[moment], carried)
        micro_index = jnp.clip(moment - phase_index, 0, micro_count - 1)
        result = run_layer(
            current,
            micro_index,
            turns,
            layer_weights,
            None if moment < 2 else whole_in,
            None if moment < 1 else whole_out,
        )
        home = moment - (pipe_count - 1)
        if moment < micro_count + pipe_count - 2:
            carried = pass_on(result, moment, micro_count)
            if home >= 0:
                out = jnp.where(phase_index == home, carried.astype(jnp.float32), out)
        else:
            out = jnp.where(phase_index == home, result, out)
    return out


def solution(mesh):
    placed = (
        P(("dp", "tensor"), None),
        P(("dp", "tensor")),
        P("dp", None),
        P("pipe", None, "tensor"),
        P("pipe", None, "tensor"),
        P("pipe", "tensor", None),
        P("pipe", None, "tensor"),
        P("pipe", None, "tensor"),
        P("pipe", "tensor", None),
        P("pipe", None),
        P("pipe", None),
    )
    return jax.shard_map(
        shards,
        mesh=mesh,
        in_specs=placed,
        out_specs=P(("dp", "pipe", "tensor"), None),
        check_vma=False,
    )
```

time: 679 us -> 592 us (0.87)
  blocking collectives: 381 us -> 240 us
  Pallas kernels: 0 us -> 52.5 us
  starting transfers between devices: 63.3 us -> 43.3 us
  between operations: 1.79 us -> 15.1 us
  local copies, waits for them, and re-layouts: 11.8 us -> 22.7 us
  matrix products: 34.8 us -> 25.7 us
  waiting for transfers between devices: 142 us -> 149 us
    all_gather x7 -> x1, blocking collectives: 121 us -> 20.8 us  [run_layer(): lax.all_gather(normalize(halfway, gain_forward), 'tensor', axis=0, tiled=...]
    all_to_all x7 -> x2, blocking collectives: 129 us -> 45.2 us  [scatter_sum(): lax.all_to_all(pair.reshape(chips, rows, -1), 'tensor', split_axis=0, con...]
    pallas_call x0 -> x5, Pallas kernels: none -> 52.5 us  [attention_half(): pl.pallas_call(attention_body, in_specs=[pl.BlockSpec(memory_space=pltpu....]
    all_gather x7 -> x8, blocking collectives: 131 us -> 174 us  [the longest x7 153 us: run_layer(): everyone = lax.all_gather(current, 'tensor', axis=0, tiled=True)]
    all_gather x0 -> x2, waiting for transfers between devices: none -> 17.1 us  [the longest x1 17.1 us: whole_projections(): whole = lax.all_gather(block, 'tensor', axis=0, tiled=True)]
    unnamed x86 -> x114, local copies, waits for them, and re-layouts: 1.56 us -> 16.9 us
    ppermute x27 -> x22, starting transfers between devices: 26.5 us -> 14.3 us  [the longest x6 8.84 us: pass_on(): return lax.ppermute(result.astype(jnp.bfloat16), 'pipe', pairs)]
    another operation x15 -> x5, other arithmetic: 9.15 us -> 0.39 us  [attention_half(): jnp.stack([micro_index, parity()]).astype(jnp.int32)]
  transfers between devices with their start and end apart: 36 -> 31, of which waited for: 33 -> 28; matrix products, arithmetic and copies ran while one was open for 3% -> 7% of each run, Pallas kernels for 0% -> 0%
where the time goes in v2:
time: 592 us; the launch traced here: 582 us
  blocking collectives  240 us (41%)
  waiting for transfers between devices  149 us (25%)
  Pallas kernels  52.5 us (9%)
  starting transfers between devices  43.3 us (7%)
  other arithmetic  33.8 us (6%)
  matrix products  25.7 us (4%)
  local copies, waits for them, and re-layouts  22.7 us (4%)
  between operations  15.1 us (3%)
    all_gather x7, blocking collectives, run_layer(): everyone = lax.all_gather(current, 'tensor', axis=0, tiled=True)  153 us
    all_to_all x6, waiting for transfers between devices, scatter_sum(): lax.all_to_all(pair.reshape(chips, rows, -1), 'tensor', split_axis=0, con...  92.8 us
    pallas_call x5, Pallas kernels, attention_half(): pl.pallas_call(attention_body, in_specs=[pl.BlockSpec(memory_space=pltpu....  52.5 us
    all_to_all x2, blocking collectives, scatter_sum(): lax.all_to_all(pair.reshape(chips, rows, -1), 'tensor', split_axis=0, con...  45.2 us
    ppermute x16, waiting for transfers between devices, swapped(): return lax.ppermute(value, 'tensor', pairs)  26.8 us
    all_to_all x6, starting transfers between devices, scatter_sum(): lax.all_to_all(pair.reshape(chips, rows, -1), 'tensor', split_axis=0, con...  24.8 us
    all_gather x1, blocking collectives, run_layer(): heads = lax.all_gather(mixed, 'tensor', axis=1, tiled=True)  21 us
    all_gather x1, blocking collectives, run_layer(): lax.all_gather(normalize(halfway, gain_forward), 'tensor', axis=0, tiled=...  20.8 us
  transfers between devices with their start and end apart: 31, of which 28 were waited for; matrix products, arithmetic and copies ran while one was open for 7% of the time, Pallas kernels for 0%

profile of v2, /device:TPU:7, one launch (start us, length us, event | category | flops | bytes accessed | tf_op | source)
XLA Modules:
  0.0 581.9 jit_solution(14806702149968326655)
XLA Ops:
  29.4 28.0 %all_gather.33 = bf16[128,3072]{1,0:T(8,128)(2,1)S(1)} all-gather(bf16[8,3072]{1,0:T(8,128)(2,1)S(1)} %slice_select_fusion), channel_id=1, replica_groups=mesh['dp'=4,'pipe'=4,'tensor'=16] {'tensor'}, dimensions={0}, use_global_device_ids=true | all-gather | bytes 835584 | tf_op jit(solution)/shard_map/all_gather | solution.py:243
  63.2 22.3 %all_to_all.45 = bf16[8,8,3072]{2,1,0:T(8,128)(2,1)S(1)} all-to-all(bf16[8,8,3072]{2,1,0:T(8,128)(2,1)S(1)} %fusion.78), channel_id=1, replica_groups={{0,2,4,6,8,10,12,14},{1,3,5,7,9,11,13,15},{16,18,20,22,24,26,28,30},{17..., dimensions={0} | all-to-all | bytes 786432 | tf_op jit(solution)/shard_map/all_to_all | solution.py:34
  85.8 20.8 %all_gather.34 = bf16[128,3072]{1,0:T(8,128)(2,1)S(1)} all-gather(bf16[8,3072]{1,0:T(8,128)(2,1)S(1)} %multiply_convert_fusion.11), channel_id=1, replica_groups=mesh['dp'=4,'pipe'=4,'tensor'=16] {'tensor'}, dimensions={0}, use_global_device_ids=true | all-gather | bytes 835584 | tf_op jit(solution)/shard_map/all_gather | solution.py:261
  111.6 23.0 %all_to_all.46 = bf16[8,8,3072]{2,1,0:T(8,128)(2,1)S(1)} all-to-all(bf16[8,8,3072]{2,1,0:T(8,128)(2,1)S(1)} %fusion.79), channel_id=1, replica_groups={{0,2,4,6,8,10,12,14},{1,3,5,7,9,11,13,15},{16,18,20,22,24,26,28,30},{17..., dimensions={0} | all-to-all | bytes 786432 | tf_op jit(solution)/shard_map/all_to_all | solution.py:34
  139.2 21.9 %all_gather.35 = bf16[128,3072]{1,0:T(8,128)(2,1)S(1)} all-gather(bf16[8,3072]{1,0:T(8,128)(2,1)S(1)} %slice_select_fusion.1), channel_id=1, replica_groups=mesh['dp'=4,'pipe'=4,'tensor'=16] {'tensor'}, dimensions={0}, use_global_device_ids=true | all-gather | bytes 835584 | tf_op jit(solution)/shard_map/all_gather | solution.py:243
  165.7 21.0 %all_gather.36 = bf16[128,2048]{1,0:T(8,128)(2,1)} all-gather(bf16[128,128]{1,0:T(8,128)(2,1)S(1)} %convolution_convert_fusion.2), channel_id=1, replica_groups=mesh['dp'=4,'pipe'=4,'tensor'=16] {'tensor'}, dimensions={1}, use_global_device_ids=true | all-gather | bytes 557056 | tf_op jit(solution)/shard_map/all_gather | solution.py:252
  186.6 7.3 %multiply_reduce_fusion.5 = (f32[128]{0:T(128)S(1)}, f32[128,3072]{1,0:T(8,128)S(1)}) fusion(bf16[128,2048]{1,0:T(8,128)(2,1)} %all_gather.36, bf16[1,2048,3072]{2,1,0:T(8,128)(2,1)} %all-gather.6.cloned.1.call-done, bf16[128,3072]{1,0:T(8,128)(2,1)} %copy-done.32), kind=kOutput, calls=%fused_computation.76 | convolution fusion | flops 1612185472 | bytes 15467008 | tf_op jit(solution)/shard_map/dot_general | solution.py:253
  206.8 16.9 %all-to-all-done.3 = bf16[8,8,3072]{2,1,0:T(8,128)(2,1)} async-done(((bf16[8,8,3072]{2,1,0:T(8,128)(2,1)}), bf16[8,8,3072]{2,1,0:T(8,128)(2,1)}, u32[]{:S(2)}, u32[]{:S(2)}) %all-to-all-start.3) | async-done | bytes 393248 | tf_op jit(solution)/shard_map/all_to_all | solution.py:34
  227.3 23.5 %all_gather.38.x_ref = bf16[128,3072]{1,0:T(8,128)(2,1)} all-gather(bf16[8,3072]{1,0:T(8,128)(2,1)S(1)} %slice_select_fusion.2), channel_id=1, replica_groups=mesh['dp'=4,'pipe'=4,'tensor'=16] {'tensor'}, dimensions={0}, use_global_device_ids=true | all-gather | bytes 835584 | tf_op jit(solution)/shard_map/all_gather | solution.py:243
  250.8 17.1 %all-gather.4.cloned.1.call-done = bf16[24576,512]{1,0:T(8,128)(2,1)} async-done(((bf16[1536,512]{1,0:T(8,128)(2,1)}), bf16[24576,512]{1,0:T(8,128)(2,1)}) %all-gather.4.cloned.1.call-update) | async-done | bytes 25165840 | tf_op jit(solution)/shard_map/all_gather | solution.py:113
  269.8 10.5 %shard_map.109 = bf16[128,3072]{1,0:T(8,128)(2,1)S(1)} custom-call(s32[2]{0:T(128)S(1)} %pad_add_fusion.where_ref, bf16[128,3072]{1,0:T(8,128)(2,1)} %all_gather.38.x_ref, f32[1,3072]{1,0:T(1,128)S(1)} %copy-done.11, f32[4,128,128]{2,1,0:T(8,128)S(1)} %copy-done.1, f32[4,128,128]{2,1,0:T(8,128)S(1)} %copy-done.6, ...), custom_call_target="tpu_custom_call" | custom-call | flops 2415919104 | bytes 18874368 | tf_op jit(solution)/shard_map/pallas_call | solution.py:203
  293.9 15.3 %all-to-all-done.4 = bf16[8,8,3072]{2,1,0:T(8,128)(2,1)} async-done(((bf16[8,8,3072]{2,1,0:T(8,128)(2,1)}), bf16[8,8,3072]{2,1,0:T(8,128)(2,1)}, u32[]{:S(2)}, u32[]{:S(2)}) %all-to-all-start.4) | async-done | bytes 393248 | tf_op jit(solution)/shard_map/all_to_all | solution.py:34
  316.8 19.9 %all_gather.40.x_ref = bf16[128,3072]{1,0:T(8,128)(2,1)} all-gather(bf16[8,3072]{1,0:T(8,128)(2,1)S(1)} %slice_select_fusion.3), channel_id=1, replica_groups=mesh['dp'=4,'pipe'=4,'tensor'=16] {'tensor'}, dimensions={0}, use_global_device_ids=true | all-gather | bytes 835584 | tf_op jit(solution)/shard_map/all_gather | solution.py:243
  336.7 10.5 %shard_map.110 = bf16[128,3072]{1,0:T(8,128)(2,1)S(1)} custom-call(s32[2]{0:T(128)S(1)} %pad_add_fusion.1.where_ref, bf16[128,3072]{1,0:T(8,128)(2,1)} %all_gather.40.x_ref, f32[1,3072]{1,0:T(1,128)S(1)} %copy-done.11, f32[4,128,128]{2,1,0:T(8,128)S(1)} %copy-done.2, f32[4,128,128]{2,1,0:T(8,128)S(1)} %copy-done.7, ...), custom_call_target="tpu_custom_call" | custom-call | flops 2415919104 | bytes 18874368 | tf_op jit(solution)/shard_map/pallas_call | solution.py:203
  360.6 15.2 %all-to-all-done.5 = bf16[8,8,3072]{2,1,0:T(8,128)(2,1)} async-done(((bf16[8,8,3072]{2,1,0:T(8,128)(2,1)}), bf16[8,8,3072]{2,1,0:T(8,128)(2,1)}, u32[]{:S(2)}, u32[]{:S(2)}) %all-to-all-start.5) | async-done | bytes 393248 | tf_op jit(solution)/shard_map/all_to_all | solution.py:34
  380.8 19.7 %all_gather.41.x_ref = bf16[128,3072]{1,0:T(8,128)(2,1)} all-gather(bf16[8,3072]{1,0:T(8,128)(2,1)S(1)} %collective-permute-done.13), channel_id=1, replica_groups=mesh['dp'=4,'pipe'=4,'tensor'=16] {'tensor'}, dimensions={0}, use_global_device_ids=true | all-gather | bytes 835584 | tf_op jit(solution)/shard_map/all_gather | solution.py:243
  400.5 10.5 %shard_map.111 = bf16[128,3072]{1,0:T(8,128)(2,1)S(1)} custom-call(s32[2]{0:T(128)S(1)} %pad_add_fusion.2.where_ref, bf16[128,3072]{1,0:T(8,128)(2,1)} %all_gather.41.x_ref, f32[1,3072]{1,0:T(1,128)S(1)} %copy-done.11, f32[4,128,128]{2,1,0:T(8,128)S(1)} %copy-done.3, f32[4,128,128]{2,1,0:T(8,128)S(1)} %copy-done.8, ...), custom_call_target="tpu_custom_call" | custom-call | flops 2415919104 | bytes 18874368 | tf_op jit(solution)/shard_map/pallas_call | solution.py:203
  424.6 15.2 %all-to-all-done.6 = bf16[8,8,3072]{2,1,0:T(8,128)(2,1)} async-done(((bf16[8,8,3072]{2,1,0:T(8,128)(2,1)}), bf16[8,8,3072]{2,1,0:T(8,128)(2,1)}, u32[]{:S(2)}, u32[]{:S(2)}) %all-to-all-start.6) | async-done | bytes 393248 | tf_op jit(solution)/shard_map/all_to_all | solution.py:34
  446.7 19.7 %all_gather.42.x_ref = bf16[128,3072]{1,0:T(8,128)(2,1)} all-gather(bf16[8,3072]{1,0:T(8,128)(2,1)S(1)} %collective-permute-done.16), channel_id=1, replica_groups=mesh['dp'=4,'pipe'=4,'tensor'=16] {'tensor'}, dimensions={0}, use_global_device_ids=true | all-gather | bytes 835584 | tf_op jit(solution)/shard_map/all_gather | solution.py:243
  466.4 10.5 %shard_map.112 = bf16[128,3072]{1,0:T(8,128)(2,1)S(1)} custom-call(s32[2]{0:T(128)S(1)} %pad_add_fusion.3.where_ref, bf16[128,3072]{1,0:T(8,128)(2,1)} %all_gather.42.x_ref, f32[1,3072]{1,0:T(1,128)S(1)} %copy-done.11, f32[4,128,128]{2,1,0:T(8,128)S(1)} %copy-done.4, f32[4,128,128]{2,1,0:T(8,128)S(1)} %copy-done.9, ...), custom_call_target="tpu_custom_call" | custom-call | flops 2415919104 | bytes 18874368 | tf_op jit(solution)/shard_map/pallas_call | solution.py:203
  490.3 15.2 %all-to-all-done.7 = bf16[8,8,3072]{2,1,0:T(8,128)(2,1)} async-done(((bf16[8,8,3072]{2,1,0:T(8,128)(2,1)}), bf16[8,8,3072]{2,1,0:T(8,128)(2,1)}, u32[]{:S(2)}, u32[]{:S(2)}) %all-to-all-start.7) | async-done | bytes 393248 | tf_op jit(solution)/shard_map/all_to_all | solution.py:34
  512.9 19.9 %all_gather.43.x_ref = bf16[128,3072]{1,0:T(8,128)(2,1)} all-gather(bf16[8,3072]{1,0:T(8,128)(2,1)S(1)} %collective-permute-done.19), channel_id=1, replica_groups=mesh['dp'=4,'pipe'=4,'tensor'=16] {'tensor'}, dimensions={0}, use_global_device_ids=true | all-gather | bytes 835584 | tf_op jit(solution)/shard_map/all_gather | solution.py:243
  532.9 10.5 %shard_map.113 = bf16[128,3072]{1,0:T(8,128)(2,1)S(1)} custom-call(s32[2]{0:T(128)S(1)} %pad_add_fusion.4.where_ref, bf16[128,3072]{1,0:T(8,128)(2,1)} %all_gather.43.x_ref, f32[1,3072]{1,0:T(1,128)S(1)} %copy-done.11, f32[4,128,128]{2,1,0:T(8,128)S(1)} %copy-done.5, f32[4,128,128]{2,1,0:T(8,128)S(1)} %copy-done.10, ...), custom_call_target="tpu_custom_call" | custom-call | flops 2415919104 | bytes 18874368 | tf_op jit(solution)/shard_map/pallas_call | solution.py:203
  556.8 15.2 %all-to-all-done.8 = bf16[8,8,3072]{2,1,0:T(8,128)(2,1)} async-done(((bf16[8,8,3072]{2,1,0:T(8,128)(2,1)}), bf16[8,8,3072]{2,1,0:T(8,128)(2,1)}, u32[]{:S(2)}, u32[]{:S(2)}) %all-to-all-start.8) | async-done | bytes 393248 | tf_op jit(solution)/shard_map/all_to_all | solution.py:34
  (303 shorter events, 157.6 us)
Async XLA Ops:
  6.5 180.1 %all-gather.6.cloned.1.call-start = ((), (), s32[]{:S(2)}) async-start(), calls=%async_computation.10 | async-start | bytes 13369344 | tf_op jit(solution)/shard_map/all_gather | solution.py:324
  7.3 260.7 %all-gather.4.cloned.1.call-start = ((), (), s32[]{:S(2)}) async-start(), calls=%async_computation.9 | async-start | bytes 26738688 | tf_op jit(solution)/shard_map/all_gather | solution.py:113
  9.4 2.7 collective-permute-start.7
  15.6 11.7 %all-to-all-start = ((bf16[4,16,3200]{2,1,0:T(8,128)(2,1)}), bf16[4,16,3200]{2,1,0:T(8,128)(2,1)}, u32[]{:S(2)}, u32[]{:S(2)}) async-start(bf16[4,16,3200]{2,1,0:T(8,128)(2,1)} %bitcast.317), calls=%async_computation | async-start | bytes 819200 | tf_op jit(solution)/shard_map/all_to_all | solution.py:293
  61.4 1.8 collective-permute-start.1
  109.8 1.8 collective-permute-start.2
  134.7 3.6 collective-permute-start.3
  197.8 1.8 collective-permute-start.5
  200.5 23.2 %all-to-all-start.3 = ((bf16[8,8,3072]{2,1,0:T(8,128)(2,1)}), bf16[8,8,3072]{2,1,0:T(8,128)(2,1)}, u32[]{:S(2)}, u32[]{:S(2)}) async-start(bf16[8,8,3072]{2,1,0:T(8,128)(2,1)} %fusion.80), calls=%async_computation.3 | async-start | bytes 786432 | tf_op jit(solution)/shard_map/all_to_all | solution.py:34
  280.3 2.4 collective-permute-start.8
  287.0 1.8 collective-permute-start.9
  289.6 19.6 %all-to-all-start.4 = ((bf16[8,8,3072]{2,1,0:T(8,128)(2,1)}), bf16[8,8,3072]{2,1,0:T(8,128)(2,1)}, u32[]{:S(2)}, u32[]{:S(2)}) async-start(bf16[8,8,3072]{2,1,0:T(8,128)(2,1)} %fusion.81), calls=%async_computation.4 | async-start | bytes 786432 | tf_op jit(solution)/shard_map/all_to_all | solution.py:34
  311.2 4.8 collective-permute-start.10
  347.2 2.4 collective-permute-start.11
  356.5 19.3 %all-to-all-start.5 = ((bf16[8,8,3072]{2,1,0:T(8,128)(2,1)}), bf16[8,8,3072]{2,1,0:T(8,128)(2,1)}, u32[]{:S(2)}, u32[]{:S(2)}) async-start(bf16[8,8,3072]{2,1,0:T(8,128)(2,1)} %fusion.82), calls=%async_computation.5 | async-start | bytes 786432 | tf_op jit(solution)/shard_map/all_to_all | solution.py:34
  377.8 3.0 collective-permute-start.13
  411.1 2.6 collective-permute-start.14
  420.5 19.3 %all-to-all-start.6 = ((bf16[8,8,3072]{2,1,0:T(8,128)(2,1)}), bf16[8,8,3072]{2,1,0:T(8,128)(2,1)}, u32[]{:S(2)}, u32[]{:S(2)}) async-start(bf16[8,8,3072]{2,1,0:T(8,128)(2,1)} %fusion.83), calls=%async_computation.6 | async-start | bytes 786432 | tf_op jit(solution)/shard_map/all_to_all | solution.py:34
  441.9 4.8 collective-permute-start.16
  476.9 2.4 collective-permute-start.17
  486.2 19.3 %all-to-all-start.7 = ((bf16[8,8,3072]{2,1,0:T(8,128)(2,1)}), bf16[8,8,3072]{2,1,0:T(8,128)(2,1)}, u32[]{:S(2)}, u32[]{:S(2)}) async-start(bf16[8,8,3072]{2,1,0:T(8,128)(2,1)} %fusion.84), calls=%async_computation.7 | async-start | bytes 786432 | tf_op jit(solution)/shard_map/all_to_all | solution.py:34
  507.5 4.8 collective-permute-start.19
  543.4 2.4 collective-permute-start.20
  552.7 19.3 %all-to-all-start.8 = ((bf16[8,8,3072]{2,1,0:T(8,128)(2,1)}), bf16[8,8,3072]{2,1,0:T(8,128)(2,1)}, u32[]{:S(2)}, u32[]{:S(2)}) async-start(bf16[8,8,3072]{2,1,0:T(8,128)(2,1)} %fusion.85), calls=%async_computation.8 | async-start | bytes 786432 | tf_op jit(solution)/shard_map/all_to_all | solution.py:34
  (64 other events, 775.0 us)
Sparse Core Ops, SparseCore 0:
  9.2 94.5 all-gather.5
  105.6 162.3 all-gather.3

commit v3 on v2

--- a/solution.py
+++ b/solution.py
@@ -7,7 +7,9 @@
 
 HD = 128
 CORES = 2
-VMEM_LIMIT = 52 * 2**20
+VMEM_LIMIT = 48 * 2**20
+UNIT = 128
+PLAIN_MOMENTS = 2
 
 
 def swapped(value):
@@ -19,7 +21,7 @@
     return lax.axis_index("tensor") % CORES
 
 
-def scatter_sum(left, weight):
+def scatter_add(total, left, weight):
     peers = lax.axis_size("tensor")
     chips = peers // CORES
     rows = left.shape[0] // peers
@@ -39,7 +41,9 @@
         tiled=True,
         axis_index_groups=[list(range(core, peers, CORES)) for core in range(CORES)],
     )
-    return jnp.sum(blocks.astype(jnp.float32), axis=0)
+    for chip in range(chips):
+        total = total + blocks[chip].astype(jnp.float32)
+    return total
 
 
 def tables(doc_ids):
@@ -51,10 +55,13 @@
     frequency = 500000.0 ** (-(jnp.arange(half, dtype=jnp.float32) * 2.0 / HD))
     angles = places[:, :, None] * frequency
     cosine, sine = jnp.cos(angles), jnp.sin(angles)
-    return (
-        jnp.concatenate([cosine, cosine], axis=-1),
-        jnp.concatenate([-sine, sine], axis=-1),
-        seen.astype(jnp.float32),
+    return jnp.stack(
+        [
+            jnp.concatenate([cosine, cosine], axis=-1),
+            jnp.concatenate([-sine, sine], axis=-1),
+            seen.astype(jnp.float32),
+        ],
+        axis=1,
     )
 
 
@@ -99,30 +106,32 @@
     return attend(queries, keys, values, seen)
 
 
-def whole_projections(query_local, pair_local):
-    both = jnp.concatenate([query_local, pair_local], axis=1)
-    half = both.shape[0] // 2
-    first, second = both[:half], both[half:]
-    kept = jnp.where(parity() == 0, first, second)
-    got = swapped(jnp.where(parity() == 0, second, first))
-    block = jnp.where(
-        parity() == 0,
-        jnp.concatenate([kept, got], axis=1),
-        jnp.concatenate([got, kept], axis=1),
-    )
-    whole = lax.all_gather(block, "tensor", axis=0, tiled=True)
-    return whole.reshape(-1, 2 * half, block.shape[1])
+def quarter_weights(query_local, pair_local, out_local):
+    chips, parts = lax.axis_size("tensor") // CORES, lax.axis_size("dp")
+    turn = lax.axis_index("dp")
+    width, columns = query_local.shape
+    cut, wide = width // parts, 2 * columns
+    rows_in = [
+        lax.dynamic_slice_in_dim(local, turn * cut, cut, 0) for local in (query_local, pair_local)
+    ]
+    columns_out = lax.dynamic_slice_in_dim(out_local, turn * cut, cut, 1)
+    blocks = [columns_out[:, at : at + wide] for at in range(0, cut, wide)]
+    quarter = jnp.concatenate([jnp.concatenate(rows_in, axis=1)] + blocks, axis=0)
+    column = lax.all_gather(quarter, "tensor", axis=0, tiled=True)
+    return column.reshape(chips // CORES, CORES, CORES, -1, UNIT, wide)
+
+
+def whole_weights(column):
+    return lax.all_gather(
+        lax.dynamic_index_in_dim(column, parity(), 1, keepdims=False), "dp", axis=0
+    )
 
 
 def attention_body(
-    where_ref,
     x_ref,
     gain_ref,
-    cosine_ref,
-    sine_ref,
-    seen_ref,
-    in_hbm,
-    out_hbm,
+    turns_ref,
+    whole_hbm,
     total_ref,
     normed_ref,
     in_ref,
@@ -130,23 +139,28 @@
     in_sem,
     out_sem,
 ):
-    groups = in_ref.shape[0]
+    groups, parts, units, _, columns = in_ref.shape
+    tiles, wide = out_ref.shape[1], out_ref.shape[-1]
     rows, width = x_ref.shape
-    inner = out_hbm.shape[2]
     strip = 16
-    micro, core = where_ref[0], where_ref[1]
-    fetch_in = [
-        pltpu.make_async_copy(in_hbm.at[group, core], in_ref.at[group], in_sem.at[group])
-        for group in range(groups)
-    ]
-    fetch_out = [
-        pltpu.make_async_copy(
-            out_hbm.at[group, core],
-            out_ref.at[pl.ds(group * inner, inner), :],
-            out_sem.at[group],
-        )
-        for group in range(groups)
-    ]
+    fetch_in, fetch_out = [], []
+    for group in range(groups):
+        for core in range(CORES):
+            slot = group * CORES + core
+            fetch_in.append(
+                pltpu.make_async_copy(
+                    whole_hbm.at[:, group, core, pl.ds(0, units)],
+                    in_ref.at[group, :, :, :, pl.ds(core * wide, wide)],
+                    in_sem.at[slot],
+                )
+            )
+            fetch_out.append(
+                pltpu.make_async_copy(
+                    whole_hbm.at[:, group, core, pl.ds(units, tiles)],
+                    out_ref.at[:, :, slot],
+                    out_sem.at[slot],
+                )
+            )
     for copy in fetch_in + fetch_out:
         copy.start()
 
@@ -155,15 +169,17 @@
         part = pl.ds(pl.multiple_of(index * strip, strip), strip)
         normed_ref[part, :] = normalize(x_ref[part, :].astype(jnp.float32), gain_ref[...])
 
-    cosine, sine, seen = cosine_ref[micro], sine_ref[micro], seen_ref[micro]
+    cosine, sine, seen = turns_ref[0], turns_ref[1], turns_ref[2]
     seen_twice = jnp.concatenate([seen, seen], axis=0)
 
     def turn(head):
         return head * cosine + pltpu.roll(head, HD // 2, 1) * sine
 
     def project(group):
-        fetch_in[group].wait()
-        return jnp.dot(normed_ref[...], in_ref[group], preferred_element_type=jnp.float32)
+        for core in range(CORES):
+            fetch_in[group * CORES + core].wait()
+        weight = in_ref[group].reshape(width, columns)
+        return jnp.dot(normed_ref[...], weight, preferred_element_type=jnp.float32)
 
     mixed = []
     heads = project(0)
@@ -183,52 +199,47 @@
     left = jnp.concatenate(mixed, axis=1)
     for copy in fetch_out:
         copy.wait()
-    tile = 512
-
-    @pl.loop(0, width // tile)
-    def _(index):
-        part = pl.ds(pl.multiple_of(index * tile, tile), tile)
-        total_ref[:, part] = jnp.dot(
-            left, out_ref[:, part], preferred_element_type=jnp.float32
+    for tile in range(parts * tiles):
+        right = out_ref[tile // tiles, tile % tiles].reshape(left.shape[1], wide)
+        total_ref[:, tile * wide : (tile + 1) * wide] = jnp.dot(
+            left, right, preferred_element_type=jnp.float32
         ).astype(jnp.bfloat16)
 
 
-def attention_half(everyone, micro_index, turns, whole_in, whole_out, gain):
+def attention_half(everyone, turns, whole, gain):
     rows, width = everyone.shape
-    chips, _, columns = whole_in.shape
-    groups = chips // CORES
-    inner = whole_out.shape[0] // chips
+    parts, groups, _, units, _, wide = whole.shape
+    inner = width // UNIT // parts
+    tiles = units - inner
+    slots = groups * CORES
     vmem = pl.BlockSpec(memory_space=pltpu.VMEM)
-    hbm = pl.BlockSpec(memory_space=pltpu.HBM)
     return pl.pallas_call(
         attention_body,
-        in_specs=[pl.BlockSpec(memory_space=pltpu.SMEM)] + [vmem] * 5 + [hbm] * 2,
+        in_specs=[vmem] * 3 + [pl.BlockSpec(memory_space=pltpu.HBM)],
         out_specs=vmem,
         scratch_shapes=[
             pltpu.VMEM((rows, width), jnp.bfloat16),
-            pltpu.VMEM((groups, width, columns), jnp.bfloat16),
-            pltpu.VMEM((groups * inner, width), jnp.bfloat16),
-            pltpu.SemaphoreType.DMA((groups,)),
-            pltpu.SemaphoreType.DMA((groups,)),
+            pltpu.VMEM((groups, parts, inner, UNIT, CORES * wide), jnp.bfloat16),
+            pltpu.VMEM((parts, tiles, slots, UNIT, wide), jnp.bfloat16),
+            pltpu.SemaphoreType.DMA((slots,)),
+            pltpu.SemaphoreType.DMA((slots,)),
         ],
         out_shape=jax.ShapeDtypeStruct((rows, width), jnp.bfloat16),
         compiler_params=pltpu.CompilerParams(vmem_limit_bytes=VMEM_LIMIT),
         cost_estimate=pl.CostEstimate(
-            flops=2 * rows * width * groups * (columns + inner),
-            bytes_accessed=2 * width * groups * (columns + inner),
+            flops=2 * rows * parts * slots * units * UNIT * wide,
+            bytes_accessed=2 * parts * slots * units * UNIT * wide,
             transcendentals=2 * rows * rows * groups,
         ),
     )(
-        jnp.stack([micro_index, parity()]).astype(jnp.int32),
         everyone,
         gain[None],
-        *turns,
-        whole_in.reshape(groups, CORES, width, columns),
-        whole_out.reshape(groups, CORES, inner, width),
-    )
-
-
-def run_layer(current, micro_index, turns, layer_weights, whole_in, whole_out):
+        turns,
+        whole,
+    )
+
+
+def run_layer(current, micro_index, turns, layer_weights, whole, column):
     (
         query_local,
         pair_local,
@@ -240,29 +251,28 @@
         gain_forward,
     ) = layer_weights
     slab_rows = current.shape[0]
+    now = lax.dynamic_index_in_dim(turns, micro_index, 0, keepdims=False)
     everyone = lax.all_gather(current, "tensor", axis=0, tiled=True)
-    if whole_in is not None:
-        part = attention_half(everyone, micro_index, turns, whole_in, whole_out, gain_attention)
+    if whole is not None:
+        part = attention_half(everyone, now, whole, gain_attention)
         total = part.astype(jnp.float32) + swapped(part).astype(jnp.float32)
-    else:
-        now = [lax.dynamic_index_in_dim(table, micro_index, 0, keepdims=False) for table in turns]
-        piece = normalize(everyone.astype(jnp.float32), gain_attention)
-        mixed = attend_local(piece, query_local, pair_local, now)
-        if whole_out is not None:
-            heads = lax.all_gather(mixed, "tensor", axis=1, tiled=True)
-            total = jnp.dot(heads, whole_out, preferred_element_type=jnp.float32)
-    if whole_out is not None:
         halfway_all = everyone.astype(jnp.float32) + total
         piece = normalize(halfway_all, gain_forward)
         start = lax.axis_index("tensor") * slab_rows
         halfway = lax.dynamic_slice_in_dim(halfway_all, start, slab_rows, 0)
     else:
-        halfway = current.astype(jnp.float32) + scatter_sum(mixed, out_local)
+        piece = normalize(everyone.astype(jnp.float32), gain_attention)
+        mixed = attend_local(piece, query_local, pair_local, now)
+        halfway = scatter_add(current.astype(jnp.float32), mixed, out_local)
+        if column is not None:
+            column, halfway = lax.optimization_barrier((column, halfway))
+            whole = whole_weights(column)
         piece = lax.all_gather(normalize(halfway, gain_forward), "tensor", axis=0, tiled=True)
     gate = jnp.dot(piece, gate_local, preferred_element_type=jnp.float32)
     upward = jnp.dot(piece, up_local, preferred_element_type=jnp.float32)
     hidden = (jax.nn.silu(gate) * upward).astype(jnp.bfloat16)
-    return halfway + scatter_sum(hidden, down_local)
+    result = scatter_add(halfway, hidden, down_local)
+    return result if column is None else (result, whole)
 
 
 def pass_on(result, moment, micro_count):
@@ -321,8 +331,8 @@
     micro_count, micro_rows = segments.shape
     slab_rows = micro_rows // lax.axis_size("tensor")
     width = tokens.shape[1]
-    whole_out = lax.all_gather(out_weight[0], "tensor", axis=0, tiled=True)
-    whole_in = whole_projections(query_weight[0], key_value_weight[0])
+    column = quarter_weights(query_weight[0], key_value_weight[0], out_weight[0])
+    whole = None
     regrouped = regroup(
         tokens,
         destination,
@@ -356,9 +366,11 @@
             micro_index,
             turns,
             layer_weights,
-            None if moment < 2 else whole_in,
-            None if moment < 1 else whole_out,
+            None if moment < PLAIN_MOMENTS else whole,
+            column if moment == 0 else None,
         )
+        if moment == 0:
+            result, whole = result
         home = moment - (pipe_count - 1)
         if moment < micro_count + pipe_count - 2:
             carried = pass_on(result, moment, micro_count)

time: 592 us -> 555 us (0.938)
  waiting for transfers between devices: 149 us -> 117 us
  blocking collectives: 240 us -> 266 us
  Pallas kernels: 52.5 us -> 37.5 us
  other arithmetic: 33.8 us -> 23.7 us
  starting transfers between devices: 43.3 us -> 35.2 us
    all_to_all x2 -> x5, blocking collectives: 45.2 us -> 92 us  [scatter_add(): lax.all_to_all(pair.reshape(chips, rows, -1), 'tensor', split_axis=0, con...]
    all_to_all x6 -> x4, waiting for transfers between devices: 92.8 us -> 64.6 us  [scatter_add(): lax.all_to_all(pair.reshape(chips, rows, -1), 'tensor', split_axis=0, con...]
    all_gather x1 -> x0, blocking collectives: 21 us -> none  [run_layer(): heads = lax.all_gather(mixed, 'tensor', axis=1, tiled=True)]
    pallas_call x5, Pallas kernels: 52.5 us -> 37.5 us  [attention_half(): pl.pallas_call(attention_body, in_specs=[vmem] * 3 + [pl.BlockSpec(memory...]
    dynamic_slice x0 -> x9, local copies, waits for them, and re-layouts: none -> 14.8 us  [the longest x6 7.58 us: run_layer(): now = lax.dynamic_index_in_dim(turns, micro_index, 0, keepdims=False)]
    all_gather x1 -> x2, blocking collectives: 20.8 us -> 35 us  [run_layer(): lax.all_gather(normalize(halfway, gain_forward), 'tensor', axis=0, tiled=...]
    all_gather x7, blocking collectives: 153 us -> 139 us  [run_layer(): everyone = lax.all_gather(current, 'tensor', axis=0, tiled=True)]
    all_to_all x6 -> x4, starting transfers between devices: 24.8 us -> 17.8 us  [scatter_add(): lax.all_to_all(pair.reshape(chips, rows, -1), 'tensor', split_axis=0, con...]
  transfers between devices with their start and end apart: 31 -> 29, of which waited for: 28 -> 27; matrix products, arithmetic and copies ran while one was open for 7% -> 7% of each run, Pallas kernels for 0% -> 0%
where the time goes in v3:
time: 555 us; the launch traced here: 545 us
  blocking collectives  266 us (48%)
  waiting for transfers between devices  117 us (21%)
  Pallas kernels  37.5 us (7%)
  starting transfers between devices  35.2 us (6%)
  local copies, waits for them, and re-layouts  28.1 us (5%)
  other arithmetic  23.7 us (4%)
  matrix products  22.5 us (4%)
  between operations  15 us (3%)
    all_gather x7, blocking collectives, run_layer(): everyone = lax.all_gather(current, 'tensor', axis=0, tiled=True)  139 us
    all_to_all x5, blocking collectives, scatter_add(): lax.all_to_all(pair.reshape(chips, rows, -1), 'tensor', split_axis=0, con...  92 us
    all_to_all x4, waiting for transfers between devices, scatter_add(): lax.all_to_all(pair.reshape(chips, rows, -1), 'tensor', split_axis=0, con...  64.6 us
    pallas_call x5, Pallas kernels, attention_half(): pl.pallas_call(attention_body, in_specs=[vmem] * 3 + [pl.BlockSpec(memory...  37.5 us
    all_gather x2, blocking collectives, run_layer(): lax.all_gather(normalize(halfway, gain_forward), 'tensor', axis=0, tiled=...  35 us
    ppermute x16, waiting for transfers between devices, swapped(): return lax.ppermute(value, 'tensor', pairs)  26.3 us
    all_to_all x4, starting transfers between devices, scatter_add(): lax.all_to_all(pair.reshape(chips, rows, -1), 'tensor', split_axis=0, con...  17.8 us
    all_gather x1, waiting for transfers between devices, whole_weights(): lax.all_gather(lax.dynamic_index_in_dim(column, parity(), 1, keepdims=Fal...  16.6 us
  transfers between devices with their start and end apart: 29, of which 27 were waited for; matrix products, arithmetic and copies ran while one was open for 7% of the time, Pallas kernels for 0%

profile of v3, /device:TPU:7, one launch (start us, length us, event | category | flops | bytes accessed | tf_op | source)
XLA Modules:
  0.0 544.8 jit_solution(5061796795268095475)
XLA Ops:
  25.1 28.4 %all_gather.37 = bf16[128,3072]{1,0:T(8,128)(2,1)S(1)} all-gather(bf16[8,3072]{1,0:T(8,128)(2,1)S(1)} %slice_select_fusion), channel_id=1, replica_groups=mesh['dp'=4,'pipe'=4,'tensor'=16] {'tensor'}, dimensions={0}, use_global_device_ids=true | all-gather | bytes 835584 | tf_op jit(solution)/shard_map/all_gather | solution.py:255
  65.1 19.0 %all-to-all-done.1 = bf16[8,8,3072]{2,1,0:T(8,128)(2,1)S(1)} async-done(((bf16[8,8,3072]{2,1,0:T(8,128)(2,1)}), bf16[8,8,3072]{2,1,0:T(8,128)(2,1)S(1)}, u32[]{:S(2)}, u32[]{:S(2)}) %all-to-all-start.1) | async-done | bytes 393248 | tf_op jit(solution)/shard_map/all_to_all | solution.py:36
  92.8 17.8 %all_gather.38 = bf16[128,3072]{1,0:T(8,128)(2,1)S(1)} all-gather(bf16[8,3072]{1,0:T(8,128)(2,1)S(1)} %multiply_convert_fusion.11), channel_id=1, replica_groups=mesh['dp'=4,'pipe'=4,'tensor'=16] {'tensor'}, dimensions={0}, use_global_device_ids=true | all-gather | bytes 835584 | tf_op jit(solution)/shard_map/all_gather | solution.py:270
  117.3 18.2 %all_to_all.50 = bf16[8,8,3072]{2,1,0:T(8,128)(2,1)S(1)} all-to-all(bf16[8,8,3072]{2,1,0:T(8,128)(2,1)S(1)} %fusion.84), channel_id=1, replica_groups={{0,2,4,6,8,10,12,14},{1,3,5,7,9,11,13,15},{16,18,20,22,24,26,28,30},{17..., dimensions={0} | all-to-all | bytes 786432 | tf_op jit(solution)/shard_map/all_to_all | solution.py:36
  137.1 17.9 %all_gather.39 = bf16[128,3072]{1,0:T(8,128)(2,1)S(1)} all-gather(bf16[8,3072]{1,0:T(8,128)(2,1)S(1)} %slice_select_fusion.1), channel_id=1, replica_groups=mesh['dp'=4,'pipe'=4,'tensor'=16] {'tensor'}, dimensions={0}, use_global_device_ids=true | all-gather | bytes 835584 | tf_op jit(solution)/shard_map/all_gather | solution.py:255
  162.6 18.8 %all_to_all.51 = bf16[8,8,3072]{2,1,0:T(8,128)(2,1)S(1)} all-to-all(bf16[8,8,3072]{2,1,0:T(8,128)(2,1)S(1)} %fusion.85), channel_id=1, replica_groups={{0,2,4,6,8,10,12,14},{1,3,5,7,9,11,13,15},{16,18,20,22,24,26,28,30},{17..., dimensions={0} | all-to-all | bytes 786432 | tf_op jit(solution)/shard_map/all_to_all | solution.py:36
  181.7 17.2 %all_gather.40 = bf16[128,3072]{1,0:T(8,128)(2,1)S(1)} all-gather(bf16[8,3072]{1,0:T(8,128)(2,1)S(1)} %multiply_convert_fusion.10), channel_id=1, replica_groups=mesh['dp'=4,'pipe'=4,'tensor'=16] {'tensor'}, dimensions={0}, use_global_device_ids=true | all-gather | bytes 835584 | tf_op jit(solution)/shard_map/all_gather | solution.py:270
  208.9 15.2 %all-to-all-done.4 = bf16[8,8,3072]{2,1,0:T(8,128)(2,1)} async-done(((bf16[8,8,3072]{2,1,0:T(8,128)(2,1)}), bf16[8,8,3072]{2,1,0:T(8,128)(2,1)}, u32[]{:S(2)}, u32[]{:S(2)}) %all-to-all-start.4) | async-done | bytes 393248 | tf_op jit(solution)/shard_map/all_to_all | solution.py:36
  230.0 18.5 %all_gather.41.x_ref = bf16[128,3072]{1,0:T(8,128)(2,1)} all-gather(bf16[8,3072]{1,0:T(8,128)(2,1)S(1)} %slice_select_fusion.2), channel_id=1, replica_groups=mesh['dp'=4,'pipe'=4,'tensor'=16] {'tensor'}, dimensions={0}, use_global_device_ids=true | all-gather | bytes 835584 | tf_op jit(solution)/shard_map/all_gather | solution.py:255
  248.5 16.6 %all-gather.6.cloned.1.call-done = bf16[16,1,2,9,128,256]{5,4,3,2,1,0:T(8,128)(2,1)} async-done(((bf16[4,1,2,9,128,256]{5,4,3,2,1,0:T(8,128)(2,1)}), bf16[16,1,2,9,128,256]{5,4,3,2,1,0:T(8,128)(2,1)}) %all-gather.6.cloned.1.call-update) | async-done | bytes 18874384 | tf_op jit(solution)/shard_map/all_gather | solution.py:125
  266.2 7.5 %shard_map.109 = bf16[128,3072]{1,0:T(8,128)(2,1)S(1)} custom-call(bf16[128,3072]{1,0:T(8,128)(2,1)S(1)} %copy-done.1, f32[1,3072]{1,0:T(1,128)S(1)} %copy-done.2, f32[3,128,128]{2,1,0:T(8,128)S(1)} %bitcast.707, bf16[4,4,2,9,128,256]{5,4,3,2,1,0:T(8,128)(2,1)} %bitcast.716), custom_call_target="tpu_custom_call" | custom-call | flops 2415919104 | bytes 18874368 | tf_op jit(solution)/shard_map/pallas_call | solution.py:216
  290.1 15.3 %all-to-all-done.5 = bf16[8,8,3072]{2,1,0:T(8,128)(2,1)} async-done(((bf16[8,8,3072]{2,1,0:T(8,128)(2,1)}), bf16[8,8,3072]{2,1,0:T(8,128)(2,1)}, u32[]{:S(2)}, u32[]{:S(2)}) %all-to-all-start.5) | async-done | bytes 393248 | tf_op jit(solution)/shard_map/all_to_all | solution.py:36
  312.0 18.5 %all_gather.44.x_ref = bf16[128,3072]{1,0:T(8,128)(2,1)S(1)} all-gather(bf16[8,3072]{1,0:T(8,128)(2,1)S(1)} %slice_select_fusion.3), channel_id=1, replica_groups=mesh['dp'=4,'pipe'=4,'tensor'=16] {'tensor'}, dimensions={0}, use_global_device_ids=true | all-gather | bytes 835584 | tf_op jit(solution)/shard_map/all_gather | solution.py:255
  330.5 7.5 %shard_map.110 = bf16[128,3072]{1,0:T(8,128)(2,1)S(1)} custom-call(bf16[128,3072]{1,0:T(8,128)(2,1)S(1)} %all_gather.44.x_ref, f32[1,3072]{1,0:T(1,128)S(1)} %copy-done.2, f32[3,128,128]{2,1,0:T(8,128)S(1)} %bitcast.708, bf16[4,4,2,9,128,256]{5,4,3,2,1,0:T(8,128)(2,1)} %bitcast.717), custom_call_target="tpu_custom_call" | custom-call | flops 2415919104 | bytes 18874368 | tf_op jit(solution)/shard_map/pallas_call | solution.py:216
  346.0 18.2 %all_to_all.52 = bf16[8,8,3072]{2,1,0:T(8,128)(2,1)S(1)} all-to-all(bf16[8,8,3072]{2,1,0:T(8,128)(2,1)S(1)} %fusion.88), channel_id=1, replica_groups={{0,2,4,6,8,10,12,14},{1,3,5,7,9,11,13,15},{16,18,20,22,24,26,28,30},{17..., dimensions={0} | all-to-all | bytes 786432 | tf_op jit(solution)/shard_map/all_to_all | solution.py:36
  367.3 18.4 %all_gather.45.x_ref = bf16[128,3072]{1,0:T(8,128)(2,1)S(1)} all-gather(bf16[8,3072]{1,0:T(8,128)(2,1)S(1)} %collective-permute-done.13), channel_id=1, replica_groups=mesh['dp'=4,'pipe'=4,'tensor'=16] {'tensor'}, dimensions={0}, use_global_device_ids=true | all-gather | bytes 835584 | tf_op jit(solution)/shard_map/all_gather | solution.py:255
  385.7 7.5 %shard_map.111 = bf16[128,3072]{1,0:T(8,128)(2,1)S(1)} custom-call(bf16[128,3072]{1,0:T(8,128)(2,1)S(1)} %all_gather.45.x_ref, f32[1,3072]{1,0:T(1,128)S(1)} %copy-done.2, f32[3,128,128]{2,1,0:T(8,128)S(1)} %bitcast.710, bf16[4,4,2,9,128,256]{5,4,3,2,1,0:T(8,128)(2,1)} %bitcast.718), custom_call_target="tpu_custom_call" | custom-call | flops 2415919104 | bytes 18874368 | tf_op jit(solution)/shard_map/pallas_call | solution.py:216
  401.3 18.4 %all_to_all.53 = bf16[8,8,3072]{2,1,0:T(8,128)(2,1)S(1)} all-to-all(bf16[8,8,3072]{2,1,0:T(8,128)(2,1)S(1)} %fusion.89), channel_id=1, replica_groups={{0,2,4,6,8,10,12,14},{1,3,5,7,9,11,13,15},{16,18,20,22,24,26,28,30},{17..., dimensions={0} | all-to-all | bytes 786432 | tf_op jit(solution)/shard_map/all_to_all | solution.py:36
  424.6 18.4 %all_gather.46.x_ref = bf16[128,3072]{1,0:T(8,128)(2,1)S(1)} all-gather(bf16[8,3072]{1,0:T(8,128)(2,1)S(1)} %collective-permute-done.16), channel_id=1, replica_groups=mesh['dp'=4,'pipe'=4,'tensor'=16] {'tensor'}, dimensions={0}, use_global_device_ids=true | all-gather | bytes 835584 | tf_op jit(solution)/shard_map/all_gather | solution.py:255
  443.0 7.5 %shard_map.112 = bf16[128,3072]{1,0:T(8,128)(2,1)S(1)} custom-call(bf16[128,3072]{1,0:T(8,128)(2,1)S(1)} %all_gather.46.x_ref, f32[1,3072]{1,0:T(1,128)S(1)} %copy-done.2, f32[3,128,128]{2,1,0:T(8,128)S(1)} %bitcast.711, bf16[4,4,2,9,128,256]{5,4,3,2,1,0:T(8,128)(2,1)} %bitcast.719), custom_call_target="tpu_custom_call" | custom-call | flops 2415919104 | bytes 18874368 | tf_op jit(solution)/shard_map/pallas_call | solution.py:216
  458.5 18.4 %all_to_all.54 = bf16[8,8,3072]{2,1,0:T(8,128)(2,1)S(1)} all-to-all(bf16[8,8,3072]{2,1,0:T(8,128)(2,1)S(1)} %fusion.90), channel_id=1, replica_groups={{0,2,4,6,8,10,12,14},{1,3,5,7,9,11,13,15},{16,18,20,22,24,26,28,30},{17..., dimensions={0} | all-to-all | bytes 786432 | tf_op jit(solution)/shard_map/all_to_all | solution.py:36
  481.8 18.6 %all_gather.47.x_ref = bf16[128,3072]{1,0:T(8,128)(2,1)S(1)} all-gather(bf16[8,3072]{1,0:T(8,128)(2,1)S(1)} %collective-permute-done.19), channel_id=1, replica_groups=mesh['dp'=4,'pipe'=4,'tensor'=16] {'tensor'}, dimensions={0}, use_global_device_ids=true | all-gather | bytes 835584 | tf_op jit(solution)/shard_map/all_gather | solution.py:255
  500.4 7.5 %shard_map.113 = bf16[128,3072]{1,0:T(8,128)(2,1)S(1)} custom-call(bf16[128,3072]{1,0:T(8,128)(2,1)S(1)} %all_gather.47.x_ref, f32[1,3072]{1,0:T(1,128)S(1)} %copy-done.2, f32[3,128,128]{2,1,0:T(8,128)S(1)} %bitcast.709, bf16[4,4,2,9,128,256]{5,4,3,2,1,0:T(8,128)(2,1)} %bitcast.720), custom_call_target="tpu_custom_call" | custom-call | flops 2415919104 | bytes 18874368 | tf_op jit(solution)/shard_map/pallas_call | solution.py:216
  520.7 15.2 %all-to-all-done.9 = bf16[8,8,3072]{2,1,0:T(8,128)(2,1)S(1)} async-done(((bf16[8,8,3072]{2,1,0:T(8,128)(2,1)}), bf16[8,8,3072]{2,1,0:T(8,128)(2,1)S(1)}, u32[]{:S(2)}, u32[]{:S(2)}) %all-to-all-start.9) | async-done | bytes 393248 | tf_op jit(solution)/shard_map/all_to_all | solution.py:36
  (255 shorter events, 145.5 us)
Async XLA Ops:
  6.5 80.1 %all-gather.4.cloned.1.call-start = ((), (), s32[]{:S(2)}) async-start(), calls=%async_computation.10 | async-start | bytes 10027008 | tf_op jit(solution)/shard_map/all_gather | solution.py:120
  11.0 11.3 %all-to-all-start = ((bf16[4,16,3200]{2,1,0:T(8,128)(2,1)}), bf16[4,16,3200]{2,1,0:T(8,128)(2,1)}, u32[]{:S(2)}, u32[]{:S(2)}) async-start(bf16[4,16,3200]{2,1,0:T(8,128)(2,1)} %bitcast), calls=%async_computation | async-start | bytes 819200 | tf_op jit(solution)/shard_map/all_to_all | solution.py:303
  58.9 1.8 collective-permute-start.1
  61.6 22.6 %all-to-all-start.1 = ((bf16[8,8,3072]{2,1,0:T(8,128)(2,1)}), bf16[8,8,3072]{2,1,0:T(8,128)(2,1)S(1)}, u32[]{:S(2)}, u32[]{:S(2)}) async-start(bf16[8,8,3072]{2,1,0:T(8,128)(2,1)} %fusion.83), calls=%async_computation.1 | async-start | bytes 786432 | tf_op jit(solution)/shard_map/all_to_all | solution.py:36
  65.1 200.0 %all-gather.6.cloned.1.call-start = ((), (), s32[]{:S(2)}) async-start(), calls=%async_computation.11 | async-start | bytes 23592960 | tf_op jit(solution)/shard_map/all_gather | solution.py:125
  115.4 1.8 collective-permute-start.2
  160.7 1.8 collective-permute-start.5
  202.1 1.8 collective-permute-start.6
  204.8 19.3 %all-to-all-start.4 = ((bf16[8,8,3072]{2,1,0:T(8,128)(2,1)}), bf16[8,8,3072]{2,1,0:T(8,128)(2,1)}, u32[]{:S(2)}, u32[]{:S(2)}) async-start(bf16[8,8,3072]{2,1,0:T(8,128)(2,1)} %fusion.86), calls=%async_computation.4 | async-start | bytes 786432 | tf_op jit(solution)/shard_map/all_to_all | solution.py:36
  225.1 4.0 collective-permute-start.7
  273.8 2.7 collective-permute-start.8
  280.7 1.8 collective-permute-start.9
  283.3 22.0 %all-to-all-start.5 = ((bf16[8,8,3072]{2,1,0:T(8,128)(2,1)}), bf16[8,8,3072]{2,1,0:T(8,128)(2,1)}, u32[]{:S(2)}, u32[]{:S(2)}) async-start(bf16[8,8,3072]{2,1,0:T(8,128)(2,1)} %fusion.87), calls=%async_computation.5 | async-start | bytes 786432 | tf_op jit(solution)/shard_map/all_to_all | solution.py:36
  306.4 4.8 collective-permute-start.10
  338.0 2.4 collective-permute-start.11
  344.1 1.8 collective-permute-start.12
  364.3 3.0 collective-permute-start.13
  393.2 2.6 collective-permute-start.14
  399.5 1.8 collective-permute-start.15
  419.8 4.8 collective-permute-start.16
  450.5 2.4 collective-permute-start.17
  476.9 4.8 collective-permute-start.19
  507.9 2.4 collective-permute-start.20
  517.2 18.7 %all-to-all-start.9 = ((bf16[8,8,3072]{2,1,0:T(8,128)(2,1)}), bf16[8,8,3072]{2,1,0:T(8,128)(2,1)S(1)}, u32[]{:S(2)}, u32[]{:S(2)}) async-start(bf16[8,8,3072]{2,1,0:T(8,128)(2,1)} %fusion.91), calls=%async_computation.9 | async-start | bytes 786432 | tf_op jit(solution)/shard_map/all_to_all | solution.py:36
  (39 other events, 403.3 us)
Sparse Core Ops, SparseCore 0:
  9.9 76.7 all-gather.3
  91.9 173.1 all-gather.5

commit v4 on v3

--- a/solution.py
+++ b/solution.py
@@ -7,9 +7,9 @@
 
 HD = 128
 CORES = 2
-VMEM_LIMIT = 48 * 2**20
+VMEM_LIMIT = 28 * 2**20
 UNIT = 128
-PLAIN_MOMENTS = 2
+PLAIN_MOMENTS = 1
 
 
 def swapped(value):
@@ -106,7 +106,7 @@
     return attend(queries, keys, values, seen)
 
 
-def quarter_weights(query_local, pair_local, out_local):
+def whole_weights(query_local, pair_local, out_local):
     chips, parts = lax.axis_size("tensor") // CORES, lax.axis_size("dp")
     turn = lax.axis_index("dp")
     width, columns = query_local.shape
@@ -117,17 +117,12 @@
     columns_out = lax.dynamic_slice_in_dim(out_local, turn * cut, cut, 1)
     blocks = [columns_out[:, at : at + wide] for at in range(0, cut, wide)]
     quarter = jnp.concatenate([jnp.concatenate(rows_in, axis=1)] + blocks, axis=0)
-    column = lax.all_gather(quarter, "tensor", axis=0, tiled=True)
-    return column.reshape(chips // CORES, CORES, CORES, -1, UNIT, wide)
-
-
-def whole_weights(column):
-    return lax.all_gather(
-        lax.dynamic_index_in_dim(column, parity(), 1, keepdims=False), "dp", axis=0
-    )
+    whole = lax.all_gather(quarter, ("dp", "tensor"), axis=0, tiled=True)
+    return whole.reshape(parts, chips // CORES, CORES, CORES, -1, UNIT, wide)
 
 
 def attention_body(
+    where_ref,
     x_ref,
     gain_ref,
     turns_ref,
@@ -143,20 +138,21 @@
     tiles, wide = out_ref.shape[1], out_ref.shape[-1]
     rows, width = x_ref.shape
     strip = 16
+    half = where_ref[0]
     fetch_in, fetch_out = [], []
     for group in range(groups):
         for core in range(CORES):
             slot = group * CORES + core
             fetch_in.append(
                 pltpu.make_async_copy(
-                    whole_hbm.at[:, group, core, pl.ds(0, units)],
+                    whole_hbm.at[:, group, half, core, pl.ds(0, units)],
                     in_ref.at[group, :, :, :, pl.ds(core * wide, wide)],
                     in_sem.at[slot],
                 )
             )
             fetch_out.append(
                 pltpu.make_async_copy(
-                    whole_hbm.at[:, group, core, pl.ds(units, tiles)],
+                    whole_hbm.at[:, group, half, core, pl.ds(units, tiles)],
                     out_ref.at[:, :, slot],
                     out_sem.at[slot],
                 )
@@ -208,14 +204,16 @@
 
 def attention_half(everyone, turns, whole, gain):
     rows, width = everyone.shape
-    parts, groups, _, units, _, wide = whole.shape
+    parts, groups, _, _, units, _, wide = whole.shape
     inner = width // UNIT // parts
     tiles = units - inner
     slots = groups * CORES
     vmem = pl.BlockSpec(memory_space=pltpu.VMEM)
     return pl.pallas_call(
         attention_body,
-        in_specs=[vmem] * 3 + [pl.BlockSpec(memory_space=pltpu.HBM)],
+        in_specs=[pl.BlockSpec(memory_space=pltpu.SMEM)]
+        + [vmem] * 3
+        + [pl.BlockSpec(memory_space=pltpu.HBM)],
         out_specs=vmem,
         scratch_shapes=[
             pltpu.VMEM((rows, width), jnp.bfloat16),
@@ -232,6 +230,7 @@
             transcendentals=2 * rows * rows * groups,
         ),
     )(
+        parity().astype(jnp.int32)[None],
         everyone,
         gain[None],
         turns,
@@ -239,7 +238,7 @@
     )
 
 
-def run_layer(current, micro_index, turns, layer_weights, whole, column):
+def run_layer(current, micro_index, turns, layer_weights, whole):
     (
         query_local,
         pair_local,
@@ -264,15 +263,11 @@
         piece = normalize(everyone.astype(jnp.float32), gain_attention)
         mixed = attend_local(piece, query_local, pair_local, now)
         halfway = scatter_add(current.astype(jnp.float32), mixed, out_local)
-        if column is not None:
-            column, halfway = lax.optimization_barrier((column, halfway))
-            whole = whole_weights(column)
         piece = lax.all_gather(normalize(halfway, gain_forward), "tensor", axis=0, tiled=True)
     gate = jnp.dot(piece, gate_local, preferred_element_type=jnp.float32)
     upward = jnp.dot(piece, up_local, preferred_element_type=jnp.float32)
     hidden = (jax.nn.silu(gate) * upward).astype(jnp.bfloat16)
-    result = scatter_add(halfway, hidden, down_local)
-    return result if column is None else (result, whole)
+    return scatter_add(halfway, hidden, down_local)
 
 
 def pass_on(result, moment, micro_count):
@@ -331,8 +326,7 @@
     micro_count, micro_rows = segments.shape
     slab_rows = micro_rows // lax.axis_size("tensor")
     width = tokens.shape[1]
-    column = quarter_weights(query_weight[0], key_value_weight[0], out_weight[0])
-    whole = None
+    whole = whole_weights(query_weight[0], key_value_weight[0], out_weight[0])
     regrouped = regroup(
         tokens,
         destination,
@@ -367,10 +361,7 @@
             turns,
             layer_weights,
             None if moment < PLAIN_MOMENTS else whole,
-            column if moment == 0 else None,
         )
-        if moment == 0:
-            result, whole = result
         home = moment - (pipe_count - 1)
         if moment < micro_count + pipe_count - 2:
             carried = pass_on(result, moment, micro_count)

time: 555 us -> 530 us (0.955)
  blocking collectives: 266 us -> 256 us
  Pallas kernels: 37.5 us -> 47 us
  waiting for transfers between devices: 117 us -> 111 us
    all_to_all x4 -> x3, waiting for transfers between devices: 64.6 us -> 49.6 us  [scatter_add(): lax.all_to_all(pair.reshape(chips, rows, -1), 'tensor', split_axis=0, con...]
    all_gather x2 -> x1, blocking collectives: 35 us -> 22.3 us  [run_layer(): lax.all_gather(normalize(halfway, gain_forward), 'tensor', axis=0, tiled=...]
    pallas_call x5 -> x6, Pallas kernels: 37.5 us -> 47 us  [attention_half(): pl.pallas_call(attention_body, in_specs=[pl.BlockSpec(memory_space=pltpu....]
    all_gather x2 -> x1, waiting for transfers between devices: 17.5 us -> 23.2 us  [whole_weights(): whole = lax.all_gather(quarter, ('dp', 'tensor'), axis=0, tiled=True)]
    all_to_all x4 -> x3, starting transfers between devices: 17.8 us -> 12.5 us  [scatter_add(): lax.all_to_all(pair.reshape(chips, rows, -1), 'tensor', split_axis=0, con...]
    unnamed x68 -> x54, local copies, waits for them, and re-layouts: 12.6 us -> 11.3 us
    ppermute x16 -> x15, waiting for transfers between devices: 26.3 us -> 27.3 us  [swapped(): return lax.ppermute(value, 'tensor', pairs)]
  transfers between devices with their start and end apart: 29 -> 26, of which waited for: 27 -> 24; matrix products, arithmetic and copies ran while one was open for 7% -> 5% of each run, Pallas kernels for 0% -> 0%
where the time goes in v4:
time: 530 us; the launch traced here: 521 us
  blocking collectives  256 us (48%)
  waiting for transfers between devices  111 us (21%)
  Pallas kernels  47 us (9%)
  starting transfers between devices  31 us (6%)
  local copies, waits for them, and re-layouts  22.8 us (4%)
  other arithmetic  20.3 us (4%)
  matrix products  17.6 us (3%)
  between operations  14.9 us (3%)
    all_gather x7, blocking collectives, run_layer(): everyone = lax.all_gather(current, 'tensor', axis=0, tiled=True)  141 us
    all_to_all x5, blocking collectives, scatter_add(): lax.all_to_all(pair.reshape(chips, rows, -1), 'tensor', split_axis=0, con...  92.6 us
    all_to_all x3, waiting for transfers between devices, scatter_add(): lax.all_to_all(pair.reshape(chips, rows, -1), 'tensor', split_axis=0, con...  49.6 us
    pallas_call x6, Pallas kernels, attention_half(): pl.pallas_call(attention_body, in_specs=[pl.BlockSpec(memory_space=pltpu....  47 us
    ppermute x15, waiting for transfers between devices, swapped(): return lax.ppermute(value, 'tensor', pairs)  27.3 us
    all_gather x1, waiting for transfers between devices, whole_weights(): whole = lax.all_gather(quarter, ('dp', 'tensor'), axis=0, tiled=True)  23.2 us
    all_gather x1, blocking collectives, run_layer(): lax.all_gather(normalize(halfway, gain_forward), 'tensor', axis=0, tiled=...  22.3 us
    all_to_all x3, starting transfers between devices, scatter_add(): lax.all_to_all(pair.reshape(chips, rows, -1), 'tensor', split_axis=0, con...  12.5 us
  transfers between devices with their start and end apart: 26, of which 24 were waited for; matrix products, arithmetic and copies ran while one was open for 5% of the time, Pallas kernels for 0%

profile of v4, /device:TPU:7, one launch (start us, length us, event | category | flops | bytes accessed | tf_op | source)
XLA Modules:
  0.0 521.2 jit_solution(4698494931967563904)
XLA Ops:
  24.5 27.4 %all_gather.27 = bf16[128,3072]{1,0:T(8,128)(2,1)S(1)} all-gather(bf16[8,3072]{1,0:T(8,128)(2,1)S(1)} %slice_select_fusion), channel_id=1, replica_groups=mesh['dp'=4,'pipe'=4,'tensor'=16] {'tensor'}, dimensions={0}, use_global_device_ids=true | all-gather | bytes 835584 | tf_op jit(solution)/shard_map/all_gather | solution.py:254
  59.3 19.2 %all_to_all.45 = bf16[8,8,3072]{2,1,0:T(8,128)(2,1)S(1)} all-to-all(bf16[8,8,3072]{2,1,0:T(8,128)(2,1)S(1)} %fusion.66), channel_id=1, replica_groups={{0,2,4,6,8,10,12,14},{1,3,5,7,9,11,13,15},{16,18,20,22,24,26,28,30},{17..., dimensions={0} | all-to-all | bytes 786432 | tf_op jit(solution)/shard_map/all_to_all | solution.py:36
  78.8 22.3 %all_gather.28 = bf16[128,3072]{1,0:T(8,128)(2,1)S(1)} all-gather(bf16[8,3072]{1,0:T(8,128)(2,1)S(1)} %multiply_convert_fusion.12), channel_id=1, replica_groups=mesh['dp'=4,'pipe'=4,'tensor'=16] {'tensor'}, dimensions={0}, use_global_device_ids=true | all-gather | bytes 835584 | tf_op jit(solution)/shard_map/all_gather | solution.py:266
  111.1 19.2 %all-to-all-done.2 = bf16[8,8,3072]{2,1,0:T(8,128)(2,1)} async-done(((bf16[8,8,3072]{2,1,0:T(8,128)(2,1)}), bf16[8,8,3072]{2,1,0:T(8,128)(2,1)}, u32[]{:S(2)}, u32[]{:S(2)}) %all-to-all-start.2) | async-done | bytes 393248 | tf_op jit(solution)/shard_map/all_to_all | solution.py:36
  136.2 24.1 %all_gather.29.x_ref = bf16[128,3072]{1,0:T(8,128)(2,1)} all-gather(bf16[8,3072]{1,0:T(8,128)(2,1)S(1)} %slice_select_fusion.1), channel_id=1, replica_groups=mesh['dp'=4,'pipe'=4,'tensor'=16] {'tensor'}, dimensions={0}, use_global_device_ids=true | all-gather | bytes 835584 | tf_op jit(solution)/shard_map/all_gather | solution.py:254
  160.3 23.2 %all-gather.2.cloned.1.call-done = bf16[73728,256]{1,0:T(8,128)(2,1)} async-done(((bf16[1152,256]{1,0:T(8,128)(2,1)}), bf16[73728,256]{1,0:T(8,128)(2,1)}) %all-gather.2.cloned.1.call-update) | async-done | bytes 37748752 | tf_op jit(solution)/shard_map/all_gather | solution.py:120
  184.6 7.8 %shard_map.109 = bf16[128,3072]{1,0:T(8,128)(2,1)S(1)} custom-call(s32[1]{0:T(128)} %bitcast.48.where_ref, bf16[128,3072]{1,0:T(8,128)(2,1)S(1)} %copy-done.1, f32[1,3072]{1,0:T(1,128)S(1)} %copy-done.2, f32[3,128,128]{2,1,0:T(8,128)S(1)} %bitcast.618, bf16[4,4,2,2,9,128,256]{6,5,4,3,2,1,0:T(8,128)(2,1)} %bitcast.626), custom_call_target="tpu_custom_call" | custom-call | flops 2415919104 | bytes 18874368 | tf_op jit(solution)/shard_map/pallas_call | solution.py:212
  206.0 15.3 %all-to-all-done.3 = bf16[8,8,3072]{2,1,0:T(8,128)(2,1)} async-done(((bf16[8,8,3072]{2,1,0:T(8,128)(2,1)}), bf16[8,8,3072]{2,1,0:T(8,128)(2,1)}, u32[]{:S(2)}, u32[]{:S(2)}) %all-to-all-start.3) | async-done | bytes 393248 | tf_op jit(solution)/shard_map/all_to_all | solution.py:36
  224.9 17.1 %all_gather.31.x_ref = bf16[128,3072]{1,0:T(8,128)(2,1)S(1)} all-gather(bf16[8,3072]{1,0:T(8,128)(2,1)S(1)} %slice_select_fusion.2), channel_id=1, replica_groups=mesh['dp'=4,'pipe'=4,'tensor'=16] {'tensor'}, dimensions={0}, use_global_device_ids=true | all-gather | bytes 835584 | tf_op jit(solution)/shard_map/all_gather | solution.py:254
  242.0 7.8 %shard_map.110 = bf16[128,3072]{1,0:T(8,128)(2,1)S(1)} custom-call(s32[1]{0:T(128)} %bitcast.48.where_ref, bf16[128,3072]{1,0:T(8,128)(2,1)S(1)} %all_gather.31.x_ref, f32[1,3072]{1,0:T(1,128)S(1)} %copy-done.2, f32[3,128,128]{2,1,0:T(8,128)S(1)} %bitcast.620, bf16[4,4,2,2,9,128,256]{6,5,4,3,2,1,0:T(8,128)(2,1)} %bitcast.627), custom_call_target="tpu_custom_call" | custom-call | flops 2415919104 | bytes 18874368 | tf_op jit(solution)/shard_map/pallas_call | solution.py:212
  258.0 18.2 %all_to_all.46 = bf16[8,8,3072]{2,1,0:T(8,128)(2,1)S(1)} all-to-all(bf16[8,8,3072]{2,1,0:T(8,128)(2,1)S(1)} %fusion.69), channel_id=1, replica_groups={{0,2,4,6,8,10,12,14},{1,3,5,7,9,11,13,15},{16,18,20,22,24,26,28,30},{17..., dimensions={0} | all-to-all | bytes 786432 | tf_op jit(solution)/shard_map/all_to_all | solution.py:36
  278.6 5.7 %collective-permute-done.9 = bf16[8,3072]{1,0:T(8,128)(2,1)S(1)} collective-permute-done((bf16[8,3072]{1,0:T(8,128)(2,1)S(1)}, bf16[8,3072]{1,0:T(8,128)(2,1)S(1)}, u32[]{:S(2)}, u32[]{:S(2)}) %collective-permute-start.9) | collective-permute-done | bytes 49184 | tf_op jit(solution)/shard_map/ppermute | solution.py:278
  285.2 18.1 %all_gather.32.x_ref = bf16[128,3072]{1,0:T(8,128)(2,1)S(1)} all-gather(bf16[8,3072]{1,0:T(8,128)(2,1)S(1)} %slice_select_fusion.3), channel_id=1, replica_groups=mesh['dp'=4,'pipe'=4,'tensor'=16] {'tensor'}, dimensions={0}, use_global_device_ids=true | all-gather | bytes 835584 | tf_op jit(solution)/shard_map/all_gather | solution.py:254
  303.3 7.8 %shard_map.111 = bf16[128,3072]{1,0:T(8,128)(2,1)S(1)} custom-call(s32[1]{0:T(128)} %bitcast.48.where_ref, bf16[128,3072]{1,0:T(8,128)(2,1)S(1)} %all_gather.32.x_ref, f32[1,3072]{1,0:T(1,128)S(1)} %copy-done.2, f32[3,128,128]{2,1,0:T(8,128)S(1)} %bitcast.619, bf16[4,4,2,2,9,128,256]{6,5,4,3,2,1,0:T(8,128)(2,1)} %bitcast.628), custom_call_target="tpu_custom_call" | custom-call | flops 2415919104 | bytes 18874368 | tf_op jit(solution)/shard_map/pallas_call | solution.py:212
  319.1 18.4 %all_to_all.47 = bf16[8,8,3072]{2,1,0:T(8,128)(2,1)S(1)} all-to-all(bf16[8,8,3072]{2,1,0:T(8,128)(2,1)S(1)} %fusion.70), channel_id=1, replica_groups={{0,2,4,6,8,10,12,14},{1,3,5,7,9,11,13,15},{16,18,20,22,24,26,28,30},{17..., dimensions={0} | all-to-all | bytes 786432 | tf_op jit(solution)/shard_map/all_to_all | solution.py:36
  340.8 18.3 %all_gather.33.x_ref = bf16[128,3072]{1,0:T(8,128)(2,1)S(1)} all-gather(bf16[8,3072]{1,0:T(8,128)(2,1)S(1)} %collective-permute-done.12), channel_id=1, replica_groups=mesh['dp'=4,'pipe'=4,'tensor'=16] {'tensor'}, dimensions={0}, use_global_device_ids=true | all-gather | bytes 835584 | tf_op jit(solution)/shard_map/all_gather | solution.py:254
  359.1 7.8 %shard_map.112 = bf16[128,3072]{1,0:T(8,128)(2,1)S(1)} custom-call(s32[1]{0:T(128)} %bitcast.48.where_ref, bf16[128,3072]{1,0:T(8,128)(2,1)S(1)} %all_gather.33.x_ref, f32[1,3072]{1,0:T(1,128)S(1)} %copy-done.2, f32[3,128,128]{2,1,0:T(8,128)S(1)} %bitcast.622, bf16[4,4,2,2,9,128,256]{6,5,4,3,2,1,0:T(8,128)(2,1)} %bitcast.629), custom_call_target="tpu_custom_call" | custom-call | flops 2415919104 | bytes 18874368 | tf_op jit(solution)/shard_map/pallas_call | solution.py:212
  374.9 18.4 %all_to_all.48 = bf16[8,8,3072]{2,1,0:T(8,128)(2,1)S(1)} all-to-all(bf16[8,8,3072]{2,1,0:T(8,128)(2,1)S(1)} %fusion.71), channel_id=1, replica_groups={{0,2,4,6,8,10,12,14},{1,3,5,7,9,11,13,15},{16,18,20,22,24,26,28,30},{17..., dimensions={0} | all-to-all | bytes 786432 | tf_op jit(solution)/shard_map/all_to_all | solution.py:36
  399.1 18.1 %all_gather.34.x_ref = bf16[128,3072]{1,0:T(8,128)(2,1)S(1)} all-gather(bf16[8,3072]{1,0:T(8,128)(2,1)S(1)} %collective-permute-done.15), channel_id=1, replica_groups=mesh['dp'=4,'pipe'=4,'tensor'=16] {'tensor'}, dimensions={0}, use_global_device_ids=true | all-gather | bytes 835584 | tf_op jit(solution)/shard_map/all_gather | solution.py:254
  417.2 7.8 %shard_map.113 = bf16[128,3072]{1,0:T(8,128)(2,1)S(1)} custom-call(s32[1]{0:T(128)} %bitcast.48.where_ref, bf16[128,3072]{1,0:T(8,128)(2,1)S(1)} %all_gather.34.x_ref, f32[1,3072]{1,0:T(1,128)S(1)} %copy-done.2, f32[3,128,128]{2,1,0:T(8,128)S(1)} %bitcast.623, bf16[4,4,2,2,9,128,256]{6,5,4,3,2,1,0:T(8,128)(2,1)} %bitcast.630), custom_call_target="tpu_custom_call" | custom-call | flops 2415919104 | bytes 18874368 | tf_op jit(solution)/shard_map/pallas_call | solution.py:212
  433.3 18.4 %all_to_all.49 = bf16[8,8,3072]{2,1,0:T(8,128)(2,1)S(1)} all-to-all(bf16[8,8,3072]{2,1,0:T(8,128)(2,1)S(1)} %fusion.72), channel_id=1, replica_groups={{0,2,4,6,8,10,12,14},{1,3,5,7,9,11,13,15},{16,18,20,22,24,26,28,30},{17..., dimensions={0} | all-to-all | bytes 786432 | tf_op jit(solution)/shard_map/all_to_all | solution.py:36
  457.3 18.4 %all_gather.35.x_ref = bf16[128,3072]{1,0:T(8,128)(2,1)S(1)} all-gather(bf16[8,3072]{1,0:T(8,128)(2,1)S(1)} %collective-permute-done.18), channel_id=1, replica_groups=mesh['dp'=4,'pipe'=4,'tensor'=16] {'tensor'}, dimensions={0}, use_global_device_ids=true | all-gather | bytes 835584 | tf_op jit(solution)/shard_map/all_gather | solution.py:254
  475.7 7.8 %shard_map.114 = bf16[128,3072]{1,0:T(8,128)(2,1)S(1)} custom-call(s32[1]{0:T(128)} %bitcast.48.where_ref, bf16[128,3072]{1,0:T(8,128)(2,1)S(1)} %all_gather.35.x_ref, f32[1,3072]{1,0:T(1,128)S(1)} %copy-done.2, f32[3,128,128]{2,1,0:T(8,128)S(1)} %bitcast.621, bf16[4,4,2,2,9,128,256]{6,5,4,3,2,1,0:T(8,128)(2,1)} %bitcast.631), custom_call_target="tpu_custom_call" | custom-call | flops 2415919104 | bytes 18874368 | tf_op jit(solution)/shard_map/pallas_call | solution.py:212
  497.0 15.2 %all-to-all-done.8 = bf16[8,8,3072]{2,1,0:T(8,128)(2,1)} async-done(((bf16[8,8,3072]{2,1,0:T(8,128)(2,1)}), bf16[8,8,3072]{2,1,0:T(8,128)(2,1)}, u32[]{:S(2)}, u32[]{:S(2)}) %all-to-all-start.8) | async-done | bytes 393248 | tf_op jit(solution)/shard_map/all_to_all | solution.py:36
  (215 shorter events, 124.4 us)
Async XLA Ops:
  6.5 176.9 %all-gather.2.cloned.1.call-start = ((), (), s32[]{:S(2)}) async-start(), calls=%async_computation.9 | async-start | bytes 38338560 | tf_op jit(solution)/shard_map/all_gather | solution.py:120
  11.0 11.3 %all-to-all-start = ((bf16[4,16,3200]{2,1,0:T(8,128)(2,1)}), bf16[4,16,3200]{2,1,0:T(8,128)(2,1)}, u32[]{:S(2)}, u32[]{:S(2)}) async-start(bf16[4,16,3200]{2,1,0:T(8,128)(2,1)} %bitcast.645), calls=%async_computation | async-start | bytes 819200 | tf_op jit(solution)/shard_map/all_to_all | solution.py:298
  57.4 1.8 collective-permute-start.1
  104.3 1.8 collective-permute-start.2
  106.9 23.3 %all-to-all-start.2 = ((bf16[8,8,3072]{2,1,0:T(8,128)(2,1)}), bf16[8,8,3072]{2,1,0:T(8,128)(2,1)}, u32[]{:S(2)}, u32[]{:S(2)}) async-start(bf16[8,8,3072]{2,1,0:T(8,128)(2,1)} %fusion.67), calls=%async_computation.2 | async-start | bytes 786432 | tf_op jit(solution)/shard_map/all_to_all | solution.py:36
  131.2 4.1 collective-permute-start.3
  192.4 2.4 collective-permute-start.4
  199.1 1.8 collective-permute-start.5
  201.7 19.6 %all-to-all-start.3 = ((bf16[8,8,3072]{2,1,0:T(8,128)(2,1)}), bf16[8,8,3072]{2,1,0:T(8,128)(2,1)}, u32[]{:S(2)}, u32[]{:S(2)}) async-start(bf16[8,8,3072]{2,1,0:T(8,128)(2,1)} %fusion.68), calls=%async_computation.3 | async-start | bytes 786432 | tf_op jit(solution)/shard_map/all_to_all | solution.py:36
  249.9 2.5 collective-permute-start.7
  256.1 1.8 collective-permute-start.8
  276.3 8.1 %collective-permute-start.9 = (bf16[8,3072]{1,0:T(8,128)(2,1)S(1)}, bf16[8,3072]{1,0:T(8,128)(2,1)S(1)}, u32[]{:S(2)}, u32[]{:S(2)}) collective-permute-start(bf16[8,3072]{1,0:T(8,128)(2,1)S(1)} %fusion.108), channel_id=1, source_target_pairs={{0,16},{16,32},{32,48},{1,17},{17,33},{33,49},{2,18},{18,34},{34,5... | collective-permute-start | bytes 147464 | tf_op jit(solution)/shard_map/ppermute | solution.py:278
  311.1 2.4 collective-permute-start.10
  317.2 1.8 collective-permute-start.11
  337.5 3.3 collective-permute-start.12
  367.0 2.4 collective-permute-start.13
  373.0 1.8 collective-permute-start.14
  393.4 5.8 %collective-permute-start.15 = (bf16[8,3072]{1,0:T(8,128)(2,1)S(1)}, bf16[8,3072]{1,0:T(8,128)(2,1)S(1)}, u32[]{:S(2)}, u32[]{:S(2)}) collective-permute-start(bf16[8,3072]{1,0:T(8,128)(2,1)S(1)} %fusion.106), channel_id=1, source_target_pairs={{16,32},{32,48},{48,16},{17,33},{33,49},{49,17},{18,34},{34,50},{5... | collective-permute-start | bytes 147464 | tf_op jit(solution)/shard_map/ppermute | solution.py:278
  425.1 2.6 collective-permute-start.16
  431.4 1.8 collective-permute-start.17
  452.3 5.0 collective-permute-start.18
  483.6 2.4 collective-permute-start.19
  490.2 1.8 collective-permute-start.20
  492.8 19.3 %all-to-all-start.8 = ((bf16[8,8,3072]{2,1,0:T(8,128)(2,1)}), bf16[8,8,3072]{2,1,0:T(8,128)(2,1)}, u32[]{:S(2)}, u32[]{:S(2)}) async-start(bf16[8,8,3072]{2,1,0:T(8,128)(2,1)} %fusion.73), calls=%async_computation.8 | async-start | bytes 786432 | tf_op jit(solution)/shard_map/all_to_all | solution.py:36
  (29 other events, 361.5 us)
Sparse Core Ops, SparseCore 0:
  10.1 173.2 all-gather.1

commit v5 on v4

--- a/solution.py
+++ b/solution.py
@@ -270,12 +270,17 @@
     return scatter_add(halfway, hidden, down_local)
 
 
-def pass_on(result, moment, micro_count):
+def pass_on(result, moment, micro_batches):
     last = lax.axis_size("pipe") - 1
+    micro_count = micro_batches.shape[0]
     pairs = [(i, i + 1) for i in range(last) if 0 <= moment - i < micro_count]
+    sent = result.astype(jnp.bfloat16)
     if moment >= last:
         pairs.append((last, moment - last))
-    return lax.ppermute(result.astype(jnp.bfloat16), "pipe", pairs)
+    elif moment + 1 < micro_count:
+        pairs.append((last, 0))
+        sent = jnp.where(lax.axis_index("pipe") == last, micro_batches[moment + 1], sent)
+    return lax.ppermute(sent, "pipe", pairs)
 
 
 def regroup(tokens, destination, group_count, group_span, micro_rows, slab_rows):
@@ -348,11 +353,11 @@
         forward_gain[0],
     )
     phase_index = lax.axis_index("pipe")
-    carried = jnp.zeros((slab_rows, width), jnp.bfloat16)
+    carried = micro_batches[0]
     out = jnp.zeros((slab_rows, width), jnp.float32)
     for moment in range(micro_count + pipe_count - 1):
         current = carried
-        if moment < micro_count:
+        if pipe_count <= moment < micro_count:
             current = jnp.where(phase_index == 0, micro_batches[moment], carried)
         micro_index = jnp.clip(moment - phase_index, 0, micro_count - 1)
         result = run_layer(
@@ -364,7 +369,7 @@
         )
         home = moment - (pipe_count - 1)
         if moment < micro_count + pipe_count - 2:
-            carried = pass_on(result, moment, micro_count)
+            carried = pass_on(result, moment, micro_batches)
             if home >= 0:
                 out = jnp.where(phase_index == home, carried.astype(jnp.float32), out)
         else:

time: 530 us -> 528 us (level)
  waiting for transfers between devices: 111 us -> 105 us
  starting transfers between devices: 31 us -> 36.8 us
    ppermute x6, starting transfers between devices: 11.2 us -> 17 us  [pass_on(): return lax.ppermute(sent, 'pipe', pairs)]
  transfers between devices with their start and end apart: 26 -> 26, of which waited for: 24 -> 25; matrix products, arithmetic and copies ran while one was open for 5% -> 5% of each run, Pallas kernels for 0% -> 0%
where the time goes in v5:
time: 528 us; the launch traced here: 520 us
  blocking collectives  258 us (49%)
  waiting for transfers between devices  105 us (20%)
  Pallas kernels  47 us (9%)
  starting transfers between devices  36.8 us (7%)
  local copies, waits for them, and re-layouts  22.8 us (4%)
  other arithmetic  18.7 us (4%)
  matrix products  17.6 us (3%)
  between operations  14.9 us (3%)
    all_gather x7, blocking collectives, run_layer(): everyone = lax.all_gather(current, 'tensor', axis=0, tiled=True)  143 us
    all_to_all x5, blocking collectives, scatter_add(): lax.all_to_all(pair.reshape(chips, rows, -1), 'tensor', split_axis=0, con...  92.6 us
    all_to_all x3, waiting for transfers between devices, scatter_add(): lax.all_to_all(pair.reshape(chips, rows, -1), 'tensor', split_axis=0, con...  49.6 us
    pallas_call x6, Pallas kernels, attention_half(): pl.pallas_call(attention_body, in_specs=[pl.BlockSpec(memory_space=pltpu....  47 us
    ppermute x15, waiting for transfers between devices, swapped(): return lax.ppermute(value, 'tensor', pairs)  27.3 us
    all_gather x1, blocking collectives, run_layer(): lax.all_gather(normalize(halfway, gain_forward), 'tensor', axis=0, tiled=...  22.2 us
    all_gather x1, waiting for transfers between devices, whole_weights(): whole = lax.all_gather(quarter, ('dp', 'tensor'), axis=0, tiled=True)  21.8 us
    ppermute x6, starting transfers between devices, pass_on(): return lax.ppermute(sent, 'pipe', pairs)  17 us
  transfers between devices with their start and end apart: 26, of which 25 were waited for; matrix products, arithmetic and copies ran while one was open for 5% of the time, Pallas kernels for 0%

profile of v5, /device:TPU:7, one launch (start us, length us, event | category | flops | bytes accessed | tf_op | source)
XLA Modules:
  0.0 520.1 jit_solution(9308853603335260875)
XLA Ops:
  24.5 27.4 %all_gather.27 = bf16[128,3072]{1,0:T(8,128)(2,1)S(1)} all-gather(bf16[8,3072]{1,0:T(8,128)(2,1)S(1)} %slice.472), channel_id=1, replica_groups=mesh['dp'=4,'pipe'=4,'tensor'=16] {'tensor'}, dimensions={0}, use_global_device_ids=true | all-gather | bytes 835584 | tf_op jit(solution)/shard_map/all_gather | solution.py:254
  59.3 19.2 %all_to_all.45 = bf16[8,8,3072]{2,1,0:T(8,128)(2,1)S(1)} all-to-all(bf16[8,8,3072]{2,1,0:T(8,128)(2,1)S(1)} %fusion.66), channel_id=1, replica_groups={{0,2,4,6,8,10,12,14},{1,3,5,7,9,11,13,15},{16,18,20,22,24,26,28,30},{17..., dimensions={0} | all-to-all | bytes 786432 | tf_op jit(solution)/shard_map/all_to_all | solution.py:36
  78.8 22.2 %all_gather.28 = bf16[128,3072]{1,0:T(8,128)(2,1)S(1)} all-gather(bf16[8,3072]{1,0:T(8,128)(2,1)S(1)} %multiply_convert_fusion.12), channel_id=1, replica_groups=mesh['dp'=4,'pipe'=4,'tensor'=16] {'tensor'}, dimensions={0}, use_global_device_ids=true | all-gather | bytes 835584 | tf_op jit(solution)/shard_map/all_gather | solution.py:266
  111.1 19.1 %all-to-all-done.2 = bf16[8,8,3072]{2,1,0:T(8,128)(2,1)} async-done(((bf16[8,8,3072]{2,1,0:T(8,128)(2,1)}), bf16[8,8,3072]{2,1,0:T(8,128)(2,1)}, u32[]{:S(2)}, u32[]{:S(2)}) %all-to-all-start.2) | async-done | bytes 393248 | tf_op jit(solution)/shard_map/all_to_all | solution.py:36
  137.3 24.4 %all_gather.29.x_ref = bf16[128,3072]{1,0:T(8,128)(2,1)} all-gather(bf16[8,3072]{1,0:T(8,128)(2,1)S(1)} %collective-permute-done.3), channel_id=1, replica_groups=mesh['dp'=4,'pipe'=4,'tensor'=16] {'tensor'}, dimensions={0}, use_global_device_ids=true | all-gather | bytes 835584 | tf_op jit(solution)/shard_map/all_gather | solution.py:254
  161.6 21.8 %all-gather.2.cloned.1.call-done = bf16[73728,256]{1,0:T(8,128)(2,1)} async-done(((bf16[1152,256]{1,0:T(8,128)(2,1)}), bf16[73728,256]{1,0:T(8,128)(2,1)}) %all-gather.2.cloned.1.call-update) | async-done | bytes 37748752 | tf_op jit(solution)/shard_map/all_gather | solution.py:120
  184.6 7.8 %shard_map.109 = bf16[128,3072]{1,0:T(8,128)(2,1)S(1)} custom-call(s32[1]{0:T(128)} %bitcast.48.where_ref, bf16[128,3072]{1,0:T(8,128)(2,1)S(1)} %copy-done.1, f32[1,3072]{1,0:T(1,128)S(1)} %copy-done.2, f32[3,128,128]{2,1,0:T(8,128)S(1)} %bitcast.618, bf16[4,4,2,2,9,128,256]{6,5,4,3,2,1,0:T(8,128)(2,1)} %bitcast.626), custom_call_target="tpu_custom_call" | custom-call | flops 2415919104 | bytes 18874368 | tf_op jit(solution)/shard_map/pallas_call | solution.py:212
  201.7 4.3 all-to-all-start.3
  206.0 15.3 %all-to-all-done.3 = bf16[8,8,3072]{2,1,0:T(8,128)(2,1)} async-done(((bf16[8,8,3072]{2,1,0:T(8,128)(2,1)}), bf16[8,8,3072]{2,1,0:T(8,128)(2,1)}, u32[]{:S(2)}, u32[]{:S(2)}) %all-to-all-start.3) | async-done | bytes 393248 | tf_op jit(solution)/shard_map/all_to_all | solution.py:36
  226.0 18.0 %all_gather.31.x_ref = bf16[128,3072]{1,0:T(8,128)(2,1)S(1)} all-gather(bf16[8,3072]{1,0:T(8,128)(2,1)S(1)} %collective-permute-done.6), channel_id=1, replica_groups=mesh['dp'=4,'pipe'=4,'tensor'=16] {'tensor'}, dimensions={0}, use_global_device_ids=true | all-gather | bytes 835584 | tf_op jit(solution)/shard_map/all_gather | solution.py:254
  244.0 7.8 %shard_map.110 = bf16[128,3072]{1,0:T(8,128)(2,1)S(1)} custom-call(s32[1]{0:T(128)} %bitcast.48.where_ref, bf16[128,3072]{1,0:T(8,128)(2,1)S(1)} %all_gather.31.x_ref, f32[1,3072]{1,0:T(1,128)S(1)} %copy-done.2, f32[3,128,128]{2,1,0:T(8,128)S(1)} %bitcast.620, bf16[4,4,2,2,9,128,256]{6,5,4,3,2,1,0:T(8,128)(2,1)} %bitcast.627), custom_call_target="tpu_custom_call" | custom-call | flops 2415919104 | bytes 18874368 | tf_op jit(solution)/shard_map/pallas_call | solution.py:212
  259.9 18.2 %all_to_all.46 = bf16[8,8,3072]{2,1,0:T(8,128)(2,1)S(1)} all-to-all(bf16[8,8,3072]{2,1,0:T(8,128)(2,1)S(1)} %fusion.69), channel_id=1, replica_groups={{0,2,4,6,8,10,12,14},{1,3,5,7,9,11,13,15},{16,18,20,22,24,26,28,30},{17..., dimensions={0} | all-to-all | bytes 786432 | tf_op jit(solution)/shard_map/all_to_all | solution.py:36
  283.6 18.1 %all_gather.32.x_ref = bf16[128,3072]{1,0:T(8,128)(2,1)S(1)} all-gather(bf16[8,3072]{1,0:T(8,128)(2,1)S(1)} %collective-permute-done.9), channel_id=1, replica_groups=mesh['dp'=4,'pipe'=4,'tensor'=16] {'tensor'}, dimensions={0}, use_global_device_ids=true | all-gather | bytes 835584 | tf_op jit(solution)/shard_map/all_gather | solution.py:254
  301.6 7.8 %shard_map.111 = bf16[128,3072]{1,0:T(8,128)(2,1)S(1)} custom-call(s32[1]{0:T(128)} %bitcast.48.where_ref, bf16[128,3072]{1,0:T(8,128)(2,1)S(1)} %all_gather.32.x_ref, f32[1,3072]{1,0:T(1,128)S(1)} %copy-done.2, f32[3,128,128]{2,1,0:T(8,128)S(1)} %bitcast.621, bf16[4,4,2,2,9,128,256]{6,5,4,3,2,1,0:T(8,128)(2,1)} %bitcast.628), custom_call_target="tpu_custom_call" | custom-call | flops 2415919104 | bytes 18874368 | tf_op jit(solution)/shard_map/pallas_call | solution.py:212
  317.4 18.4 %all_to_all.47 = bf16[8,8,3072]{2,1,0:T(8,128)(2,1)S(1)} all-to-all(bf16[8,8,3072]{2,1,0:T(8,128)(2,1)S(1)} %fusion.70), channel_id=1, replica_groups={{0,2,4,6,8,10,12,14},{1,3,5,7,9,11,13,15},{16,18,20,22,24,26,28,30},{17..., dimensions={0} | all-to-all | bytes 786432 | tf_op jit(solution)/shard_map/all_to_all | solution.py:36
  340.4 18.3 %all_gather.33.x_ref = bf16[128,3072]{1,0:T(8,128)(2,1)S(1)} all-gather(bf16[8,3072]{1,0:T(8,128)(2,1)S(1)} %collective-permute-done.12), channel_id=1, replica_groups=mesh['dp'=4,'pipe'=4,'tensor'=16] {'tensor'}, dimensions={0}, use_global_device_ids=true | all-gather | bytes 835584 | tf_op jit(solution)/shard_map/all_gather | solution.py:254
  358.7 7.8 %shard_map.112 = bf16[128,3072]{1,0:T(8,128)(2,1)S(1)} custom-call(s32[1]{0:T(128)} %bitcast.48.where_ref, bf16[128,3072]{1,0:T(8,128)(2,1)S(1)} %all_gather.33.x_ref, f32[1,3072]{1,0:T(1,128)S(1)} %copy-done.2, f32[3,128,128]{2,1,0:T(8,128)S(1)} %bitcast.622, bf16[4,4,2,2,9,128,256]{6,5,4,3,2,1,0:T(8,128)(2,1)} %bitcast.629), custom_call_target="tpu_custom_call" | custom-call | flops 2415919104 | bytes 18874368 | tf_op jit(solution)/shard_map/pallas_call | solution.py:212
  374.5 18.4 %all_to_all.48 = bf16[8,8,3072]{2,1,0:T(8,128)(2,1)S(1)} all-to-all(bf16[8,8,3072]{2,1,0:T(8,128)(2,1)S(1)} %fusion.71), channel_id=1, replica_groups={{0,2,4,6,8,10,12,14},{1,3,5,7,9,11,13,15},{16,18,20,22,24,26,28,30},{17..., dimensions={0} | all-to-all | bytes 786432 | tf_op jit(solution)/shard_map/all_to_all | solution.py:36
  397.8 18.4 %all_gather.34.x_ref = bf16[128,3072]{1,0:T(8,128)(2,1)S(1)} all-gather(bf16[8,3072]{1,0:T(8,128)(2,1)S(1)} %collective-permute-done.15), channel_id=1, replica_groups=mesh['dp'=4,'pipe'=4,'tensor'=16] {'tensor'}, dimensions={0}, use_global_device_ids=true | all-gather | bytes 835584 | tf_op jit(solution)/shard_map/all_gather | solution.py:254
  416.1 7.8 %shard_map.113 = bf16[128,3072]{1,0:T(8,128)(2,1)S(1)} custom-call(s32[1]{0:T(128)} %bitcast.48.where_ref, bf16[128,3072]{1,0:T(8,128)(2,1)S(1)} %all_gather.34.x_ref, f32[1,3072]{1,0:T(1,128)S(1)} %copy-done.2, f32[3,128,128]{2,1,0:T(8,128)S(1)} %bitcast.623, bf16[4,4,2,2,9,128,256]{6,5,4,3,2,1,0:T(8,128)(2,1)} %bitcast.630), custom_call_target="tpu_custom_call" | custom-call | flops 2415919104 | bytes 18874368 | tf_op jit(solution)/shard_map/pallas_call | solution.py:212
  432.2 18.4 %all_to_all.49 = bf16[8,8,3072]{2,1,0:T(8,128)(2,1)S(1)} all-to-all(bf16[8,8,3072]{2,1,0:T(8,128)(2,1)S(1)} %fusion.72), channel_id=1, replica_groups={{0,2,4,6,8,10,12,14},{1,3,5,7,9,11,13,15},{16,18,20,22,24,26,28,30},{17..., dimensions={0} | all-to-all | bytes 786432 | tf_op jit(solution)/shard_map/all_to_all | solution.py:36
  456.3 18.4 %all_gather.35.x_ref = bf16[128,3072]{1,0:T(8,128)(2,1)S(1)} all-gather(bf16[8,3072]{1,0:T(8,128)(2,1)S(1)} %collective-permute-done.18), channel_id=1, replica_groups=mesh['dp'=4,'pipe'=4,'tensor'=16] {'tensor'}, dimensions={0}, use_global_device_ids=true | all-gather | bytes 835584 | tf_op jit(solution)/shard_map/all_gather | solution.py:254
  474.6 7.8 %shard_map.114 = bf16[128,3072]{1,0:T(8,128)(2,1)S(1)} custom-call(s32[1]{0:T(128)} %bitcast.48.where_ref, bf16[128,3072]{1,0:T(8,128)(2,1)S(1)} %all_gather.35.x_ref, f32[1,3072]{1,0:T(1,128)S(1)} %copy-done.2, f32[3,128,128]{2,1,0:T(8,128)S(1)} %bitcast.619, bf16[4,4,2,2,9,128,256]{6,5,4,3,2,1,0:T(8,128)(2,1)} %bitcast.631), custom_call_target="tpu_custom_call" | custom-call | flops 2415919104 | bytes 18874368 | tf_op jit(solution)/shard_map/pallas_call | solution.py:212
  495.9 15.2 %all-to-all-done.8 = bf16[8,8,3072]{2,1,0:T(8,128)(2,1)} async-done(((bf16[8,8,3072]{2,1,0:T(8,128)(2,1)}), bf16[8,8,3072]{2,1,0:T(8,128)(2,1)}, u32[]{:S(2)}, u32[]{:S(2)}) %all-to-all-start.8) | async-done | bytes 393248 | tf_op jit(solution)/shard_map/all_to_all | solution.py:36
  (212 shorter events, 124.8 us)
Async XLA Ops:
  6.5 176.9 %all-gather.2.cloned.1.call-start = ((), (), s32[]{:S(2)}) async-start(), calls=%async_computation.9 | async-start | bytes 38338560 | tf_op jit(solution)/shard_map/all_gather | solution.py:120
  11.0 11.3 %all-to-all-start = ((bf16[4,16,3200]{2,1,0:T(8,128)(2,1)}), bf16[4,16,3200]{2,1,0:T(8,128)(2,1)}, u32[]{:S(2)}, u32[]{:S(2)}) async-start(bf16[4,16,3200]{2,1,0:T(8,128)(2,1)} %bitcast.645), calls=%async_computation | async-start | bytes 819200 | tf_op jit(solution)/shard_map/all_to_all | solution.py:303
  57.4 1.8 collective-permute-start.1
  104.3 1.8 collective-permute-start.2
  107.0 23.3 %all-to-all-start.2 = ((bf16[8,8,3072]{2,1,0:T(8,128)(2,1)}), bf16[8,8,3072]{2,1,0:T(8,128)(2,1)}, u32[]{:S(2)}, u32[]{:S(2)}) async-start(bf16[8,8,3072]{2,1,0:T(8,128)(2,1)} %fusion.67), calls=%async_computation.2 | async-start | bytes 786432 | tf_op jit(solution)/shard_map/all_to_all | solution.py:36
  131.2 6.0 %collective-permute-start.3 = (bf16[8,3072]{1,0:T(8,128)(2,1)S(1)}, bf16[8,3072]{1,0:T(8,128)(2,1)S(1)}, u32[]{:S(2)}, u32[]{:S(2)}) collective-permute-start(bf16[8,3072]{1,0:T(8,128)(2,1)S(1)} %fusion.119), channel_id=1, source_target_pairs={{0,16},{48,0},{1,17},{49,1},{2,18},{50,2},{3,19},{51,3},{4,20},{52... | collective-permute-start | bytes 147464 | tf_op jit(solution)/shard_map/ppermute | solution.py:283
  192.4 2.4 collective-permute-start.4
  199.1 1.8 collective-permute-start.5
  201.7 19.6 %all-to-all-start.3 = ((bf16[8,8,3072]{2,1,0:T(8,128)(2,1)}), bf16[8,8,3072]{2,1,0:T(8,128)(2,1)}, u32[]{:S(2)}, u32[]{:S(2)}) async-start(bf16[8,8,3072]{2,1,0:T(8,128)(2,1)} %fusion.68), calls=%async_computation.3 | async-start | bytes 786432 | tf_op jit(solution)/shard_map/all_to_all | solution.py:36
  222.3 3.6 collective-permute-start.6
  251.8 2.5 collective-permute-start.7
  258.1 1.8 collective-permute-start.8
  279.0 4.5 collective-permute-start.9
  309.5 2.4 collective-permute-start.10
  315.6 1.8 collective-permute-start.11
  335.9 4.5 collective-permute-start.12
  366.5 2.4 collective-permute-start.13
  372.6 1.8 collective-permute-start.14
  392.9 4.8 collective-permute-start.15
  424.0 2.6 collective-permute-start.16
  430.3 1.8 collective-permute-start.17
  451.2 5.0 collective-permute-start.18
  482.5 2.4 collective-permute-start.19
  491.8 19.3 %all-to-all-start.8 = ((bf16[8,8,3072]{2,1,0:T(8,128)(2,1)}), bf16[8,8,3072]{2,1,0:T(8,128)(2,1)}, u32[]{:S(2)}, u32[]{:S(2)}) async-start(bf16[8,8,3072]{2,1,0:T(8,128)(2,1)} %fusion.73), calls=%async_computation.8 | async-start | bytes 786432 | tf_op jit(solution)/shard_map/all_to_all | solution.py:36
  (29 other events, 413.4 us)
Sparse Core Ops, SparseCore 0:
  10.1 173.2 all-gather.1
